TPU v7x, 128 devices: a whole 4x4x4 slice. The times are simulated.
128 devices in a mesh: pipe: 2 (over y_lo), tensor: 2 (over y_hi), ctx: 32 (over x, z, core).
Axes of the slice: x: 4, y: 4 (y_hi: 2, y_lo: 2; y = y_hi * 2 + y_lo), z: 4, core: 2. Of those that a mesh axis runs over, the one named last changes fastest.
Arguments:
- inputs: bfloat16 [2, 4096, 768], P(None, 'ctx', 'tensor'), may hold values from -6 to 6
- cotangent: bfloat16 [2, 4096, 768], P(None, 'ctx', 'tensor'), may hold values from -6 to 6
- ln_gain: bfloat16 [2, 2, 768], P('pipe'), may hold values from 0.5 to 1.5
- ln_bias: bfloat16 [2, 2, 768], P('pipe'), may hold values from -1.5 to 1.5
- qkv_weight: bfloat16 [2, 3, 768, 768], P('pipe', None, None, 'tensor'), may hold values from -0.21875 to 0.21875
- qkv_bias: bfloat16 [2, 3, 768], P('pipe', None, 'tensor'), may hold values from -1.5 to 1.5
- out_weight: bfloat16 [2, 768, 768], P('pipe', 'tensor'), may hold values from -1.5 to 1.5
- out_bias: bfloat16 [2, 768], P('pipe', 'tensor'), may hold values from -1.5 to 1.5
- fc_in_weight: bfloat16 [2, 768, 3072], P('pipe', None, 'tensor'), may hold values from -0.21875 to 0.21875
- fc_in_bias: bfloat16 [2, 3072], P('pipe', 'tensor'), may hold values from -2.5 to 2.5
- fc_out_weight: bfloat16 [2, 3072, 768], P('pipe', 'tensor'), may hold values from -0.109375 to 0.109375
Outputs:
- boundary: bfloat16 [2, 2, 4096, 768], P('pipe', None, 'ctx', 'tensor')
- ln_gain_grad: float32 [2, 2, 768], P('pipe', None, 'tensor')
- ln_bias_grad: float32 [2, 2, 768], P('pipe', None, 'tensor')
- qkv_weight_grad: float32 [2, 3, 768, 768], P('pipe', None, None, 'tensor')
- qkv_bias_grad: float32 [2, 3, 768], P('pipe', None, 'tensor')
- out_weight_grad: float32 [2, 768, 768], P('pipe', 'tensor')
- out_bias_grad: float32 [2, 768], P('pipe', 'tensor')
- fc_in_weight_grad: float32 [2, 768, 3072], P('pipe', None, 'tensor')
- fc_in_bias_grad: float32 [2, 3072], P('pipe', 'tensor')
- fc_out_weight_grad: float32 [2, 3072, 768], P('pipe', 'tensor')
All inputs are finite; a program needn't handle non-finite values.
Results may differ from a plain program's by a relative error of at most 0.02.
Values may be sent and summed in bfloat16 or wider, within the bound.
A program may use at most 192 MiB of HBM per device.

v0:
```python
import jax
import jax.numpy as jnp
from jax import lax
from jax.sharding import PartitionSpec as P

HD = 64


norm_eps = 1e-05
masked_score = -1e30


def from_behind(value, axis, by):
    peers = lax.axis_size(axis)
    pairs = [(i, i + by) for i in range(peers) if 0 <= i + by < peers]
    return lax.ppermute(value, axis, pairs)


def as_sent(value):
    return jax.tree.map(lambda a: a.astype(jnp.bfloat16) if a.dtype == jnp.float32 else a, value)


def normalize(values):
    centered = values - jnp.mean(values, axis=-1, keepdims=True)
    variance = jnp.mean(centered * centered, axis=-1, keepdims=True)
    scale = lax.rsqrt(variance + norm_eps)
    return (centered * scale, scale)


def rotate(values, positions):
    rows = values.shape[0]
    split = values.reshape(rows, -1, HD)
    turned_dims = HD // 4
    half = turned_dims // 2
    freqs = 10000.0 ** (-2.0 * jnp.arange(half, dtype=jnp.float32) / turned_dims)
    angles = positions.astype(jnp.float32)[:, None] * freqs[None, :]
    cosine = jnp.cos(angles)[:, None, :]
    sine = jnp.sin(angles)[:, None, :]
    lower = split[:, :, :half]
    upper = split[:, :, half:turned_dims]
    turned = jnp.concatenate(
        [lower * cosine - upper * sine, upper * cosine + lower * sine, split[:, :, turned_dims:]],
        axis=-1,
    )
    return turned.reshape(rows, -1)


def exact_gelu(values):
    return jax.nn.gelu(values, approximate=False)


def masked_scores(query_heads, key_heads, query_pos, key_pos):
    raw = jnp.einsum("chd,shd->hcs", query_heads, key_heads, preferred_element_type=jnp.float32)
    allowed = key_pos[None, None, :] <= query_pos[None, :, None]
    return jnp.where(allowed, raw * HD ** (-0.5), masked_score)


def attend(queries, all_keys, all_values, query_pos):
    rows = queries.shape[0]
    total = all_keys.shape[0]
    key_pos = jnp.arange(total, dtype=jnp.int32)
    scores = masked_scores(
        queries.reshape(rows, -1, HD), all_keys.reshape(total, -1, HD), query_pos, key_pos
    )
    top = jnp.max(scores, axis=-1, keepdims=True)
    weights_exp = jnp.exp(scores - top)
    total_exp = jnp.sum(weights_exp, axis=-1, keepdims=True)
    probs = (weights_exp / total_exp).astype(jnp.bfloat16)
    attn = jnp.einsum(
        "hcs,shd->chd", probs, all_values.reshape(total, -1, HD), preferred_element_type=jnp.float32
    )
    log_total = (top + jnp.log(total_exp))[:, :, 0].T
    return (attn.reshape(rows, -1), log_total)


def attend_back(queries, all_keys, all_values, query_pos, log_total, delta, grad_attn):
    rows = queries.shape[0]
    total = all_keys.shape[0]
    query_heads = queries.reshape(rows, -1, HD)
    key_heads = all_keys.reshape(total, -1, HD)
    value_heads = all_values.reshape(total, -1, HD)
    grad_heads = grad_attn.reshape(rows, -1, HD)
    key_pos = jnp.arange(total, dtype=jnp.int32)
    scores = masked_scores(query_heads, key_heads, query_pos, key_pos)
    probs = jnp.exp(scores - log_total.T[:, :, None])
    prob_grad = jnp.einsum(
        "chd,shd->hcs", grad_heads, value_heads, preferred_element_type=jnp.float32
    )
    score_grad = (probs * (prob_grad - delta.T[:, :, None]) * HD ** (-0.5)).astype(jnp.bfloat16)
    query_grad = jnp.einsum(
        "hcs,shd->chd", score_grad, key_heads, preferred_element_type=jnp.float32
    ).reshape(rows, -1)
    key_grad = jnp.einsum(
        "hcs,chd->shd", score_grad, query_heads, preferred_element_type=jnp.float32
    ).reshape(total, -1)
    value_grad = jnp.einsum(
        "hcs,chd->shd", probs.astype(jnp.bfloat16), grad_heads, preferred_element_type=jnp.float32
    ).reshape(total, -1)
    return (query_grad, key_grad, value_grad)


def layer_forward(entry, query_pos, weights):
    gain, shift, qkv_w, qkv_b, out_w, out_b, in_w, in_b, down_w = weights
    whole = lax.all_gather(entry, "tensor", axis=1, tiled=True)
    normed, _ = normalize(whole.astype(jnp.float32))
    first = (normed * gain[0] + shift[0]).astype(jnp.bfloat16)
    second = (normed * gain[1] + shift[1]).astype(jnp.bfloat16)
    pre = (
        jnp.einsum("cd,jdw->jcw", first, qkv_w, preferred_element_type=jnp.float32)
        + qkv_b[:, None, :]
    )
    queries = rotate(pre[0], query_pos).astype(jnp.bfloat16)
    keys = rotate(pre[1], query_pos).astype(jnp.bfloat16)
    values = pre[2].astype(jnp.bfloat16)
    all_keys, all_values = (
        lax.all_gather(keys, "ctx", axis=0, tiled=True),
        lax.all_gather(values, "ctx", axis=0, tiled=True),
    )
    attn, log_total = attend(queries, all_keys, all_values, query_pos)
    inner = jnp.dot(second, in_w, preferred_element_type=jnp.float32) + in_b
    act_b = exact_gelu(inner).astype(jnp.bfloat16)
    partial_sum = jnp.dot(attn.astype(jnp.bfloat16), out_w, preferred_element_type=jnp.float32)
    partial_sum = partial_sum + jnp.dot(act_b, down_w, preferred_element_type=jnp.float32)
    summed = lax.psum_scatter(
        partial_sum.astype(jnp.bfloat16), "tensor", scatter_dimension=1, tiled=True
    ).astype(jnp.float32)
    result = (entry.astype(jnp.float32) + summed + out_b).astype(jnp.bfloat16)
    held = (all_keys, all_values)
    kept = (
        whole,
        first,
        second,
        queries,
        keys,
        values,
        held[0],
        held[1],
        attn,
        log_total,
        inner,
        act_b,
    )
    return (result, kept)


def layer_backward(incoming, kept, weights, query_pos, valid):
    gain, shift, qkv_w, qkv_b, out_w, out_b, in_w, in_b, down_w = weights
    (
        whole,
        first,
        second,
        queries,
        keys,
        values,
        stored_keys,
        stored_values,
        attn,
        log_total,
        inner,
        act_b,
    ) = kept
    rows = incoming.shape[0]
    grad_whole = lax.all_gather(incoming, "tensor", axis=1, tiled=True)
    g_out_w = jnp.einsum(
        "cw,cd->wd", attn.astype(jnp.bfloat16), grad_whole, preferred_element_type=jnp.float32
    )
    g_down = jnp.einsum("cf,cd->fd", act_b, grad_whole, preferred_element_type=jnp.float32)
    g_out_b = jnp.sum(incoming.astype(jnp.float32), axis=0)
    grad_attn = jnp.einsum(
        "cd,wd->cw", grad_whole, out_w, preferred_element_type=jnp.float32
    ).astype(jnp.bfloat16)
    grad_act = jnp.einsum("cd,fd->cf", grad_whole, down_w, preferred_element_type=jnp.float32)
    _, gelu_back = jax.vjp(exact_gelu, inner)
    grad_inner = gelu_back(grad_act)[0].astype(jnp.bfloat16)
    g_in_w = jnp.einsum("cd,cf->df", second, grad_inner, preferred_element_type=jnp.float32)
    g_in_b = jnp.sum(grad_inner.astype(jnp.float32), axis=0)
    grad_second = jnp.einsum("cf,df->cd", grad_inner, in_w, preferred_element_type=jnp.float32)
    delta = jnp.sum((grad_attn.astype(jnp.float32) * attn).reshape(rows, -1, HD), axis=-1)
    all_keys, all_values = (stored_keys, stored_values)
    query_grad, key_full, value_full = attend_back(
        queries, all_keys, all_values, query_pos, log_total, delta, grad_attn
    )
    key_grad, value_grad = (
        lax.psum_scatter(
            key_full.astype(jnp.bfloat16), "ctx", scatter_dimension=0, tiled=True
        ).astype(jnp.float32),
        lax.psum_scatter(
            value_full.astype(jnp.bfloat16), "ctx", scatter_dimension=0, tiled=True
        ).astype(jnp.float32),
    )
    _, turn_back = jax.vjp(lambda turned: rotate(turned, query_pos), query_grad)
    grads_pre = jnp.stack([turn_back(query_grad)[0], turn_back(key_grad)[0], value_grad]).astype(
        jnp.bfloat16
    )
    g_qkv_w = jnp.einsum("cd,jcw->jdw", first, grads_pre, preferred_element_type=jnp.float32)
    g_qkv_b = jnp.sum(grads_pre.astype(jnp.float32), axis=1)
    grad_first = jnp.einsum("jcw,jdw->cd", grads_pre, qkv_w, preferred_element_type=jnp.float32)
    normed, scale = normalize(whole.astype(jnp.float32))
    small = jnp.stack(
        [
            jnp.sum(grad_first * normed, axis=0),
            jnp.sum(grad_second * normed, axis=0),
            jnp.sum(grad_first, axis=0),
            jnp.sum(grad_second, axis=0),
        ]
    )
    small = jnp.where(valid, small, 0.0)
    grad_norm = grad_first * gain[0] + grad_second * gain[1]
    grad_x = scale * (
        grad_norm
        - jnp.mean(grad_norm, axis=-1, keepdims=True)
        - normed * jnp.mean(grad_norm * normed, axis=-1, keepdims=True)
    )
    grad_part, small_part = (
        lax.psum_scatter(
            grad_x.astype(jnp.bfloat16), "tensor", scatter_dimension=1, tiled=True
        ).astype(jnp.float32),
        lax.psum_scatter(
            small.astype(jnp.bfloat16), "tensor", scatter_dimension=1, tiled=True
        ).astype(jnp.float32),
    )
    grad_in = (incoming.astype(jnp.float32) + grad_part).astype(jnp.bfloat16)
    contrib = (g_qkv_w, g_qkv_b, g_out_w, g_out_b, g_in_w, g_in_b, g_down, small_part)
    return (grad_in, contrib)


def body(
    inputs,
    cotangent,
    ln_gain,
    ln_bias,
    qkv_weight,
    qkv_bias,
    out_weight,
    out_bias,
    fc_in_weight,
    fc_in_bias,
    fc_out_weight,
):
    section = lax.axis_index("pipe")
    first_section = section == 0
    micro = inputs.shape[0]
    rows = inputs.shape[1]
    query_pos = lax.axis_index("ctx") * rows + jnp.arange(rows, dtype=jnp.int32)
    weights = (
        ln_gain[0],
        ln_bias[0],
        qkv_weight[0],
        qkv_bias[0],
        out_weight[0],
        out_bias[0],
        fc_in_weight[0],
        fc_in_bias[0],
        fc_out_weight[0],
    )
    kept_ticks = []
    forward_out = []
    received = jnp.zeros_like(inputs[0])
    for tick in range(micro + 1):
        entry = jnp.where(first_section, inputs[min(tick, micro - 1)], received)
        result, kept = layer_forward(entry, query_pos, weights)
        kept_ticks.append(kept)
        forward_out.append(result)
        if tick < micro:
            received = from_behind(result, "pipe", 1)
    back_received = jnp.zeros_like(cotangent[0])
    backward_out = []
    totals = None
    for tick in range(micro + 1):
        kept = jax.tree.map(
            lambda early, late: jnp.where(first_section, early, late),
            kept_ticks[max(tick - 1, 0)],
            kept_ticks[min(tick + 1, micro)],
        )
        incoming = jnp.where(first_section, back_received, cotangent[min(tick, micro - 1)])
        valid = jnp.where(first_section, tick >= 1, tick <= micro - 1)
        grad_in, contrib = layer_backward(incoming, kept, weights, query_pos, valid)
        masked = tuple((jnp.where(valid, term, 0.0) for term in contrib))
        totals = masked if totals is None else tuple((a + b for a, b in zip(totals, masked)))
        backward_out.append(grad_in)
        if tick < micro:
            back_received = from_behind(grad_in, "pipe", -1)
    summed = jax.tree.map(lambda part: part.astype(jnp.float32), lax.psum(as_sent(totals), "ctx"))
    g_qkv_w, g_qkv_b, g_out_w, g_out_b, g_in_w, g_in_b, g_down, small = summed
    boundary = jnp.stack(
        [jnp.where(first_section, backward_out[m + 1], forward_out[m + 1]) for m in range(micro)]
    )[None]
    return (
        boundary,
        small[None, 0:2],
        small[None, 2:4],
        g_qkv_w[None],
        g_qkv_b[None],
        g_out_w[None],
        g_out_b[None],
        g_in_w[None],
        g_in_b[None],
        g_down[None],
    )


def solution(mesh):
    return jax.shard_map(
        body,
        mesh=mesh,
        in_specs=(
            P(None, "ctx", "tensor"),
            P(None, "ctx", "tensor"),
            P("pipe", None, None),
            P("pipe", None, None),
            P("pipe", None, None, "tensor"),
            P("pipe", None, "tensor"),
            P("pipe", "tensor", None),
            P("pipe", "tensor"),
            P("pipe", None, "tensor"),
            P("pipe", "tensor"),
            P("pipe", "tensor", None),
        ),
        out_specs=(
            P("pipe", None, "ctx", "tensor"),
            P("pipe", None, "tensor"),
            P("pipe", None, "tensor"),
            P("pipe", None, None, "tensor"),
            P("pipe", None, "tensor"),
            P("pipe", "tensor", None),
            P("pipe", "tensor"),
            P("pipe", None, "tensor"),
            P("pipe", "tensor"),
            P("pipe", "tensor", None),
        ),
        check_vma=False,
    )
```

profile of v0, /device:TPU:1, one launch (start us, length us, event | category | flops | bytes accessed | tf_op | source)
XLA Modules:
  0.0 1370.9 jit_solution(7124494055407792015)
XLA Ops:
  31.1 45.4 %all-gather.12.cloned.1.call-done = bf16[4096,384]{0,1:T(8,128)(2,1)} async-done(((bf16[128,384]{0,1:T(8,128)(2,1)}), bf16[4096,384]{0,1:T(8,128)(2,1)}) %all-gather.12.cloned.1.call-update) | async-done | bytes 3145744 | tf_op jit(solution)/shard_map/all_gather | solution.py:116
  88.9 35.1 %all-gather.18.cloned.1.call-done = bf16[1,4096,384]{2,1,0:T(8,128)(2,1)} async-done(((bf16[1,128,384]{2,1,0:T(8,128)(2,1)}), bf16[1,4096,384]{2,1,0:T(8,128)(2,1)}) %all-gather.18.cloned.1.call-update) | async-done | bytes 3145744 | tf_op jit(solution)/shard_map/all_gather | solution.py:117
  128.6 9.8 fusion.361
  141.8 13.9 %reduce-scatter.46.cloned.1.call-done = bf16[384,128]{1,0:T(8,128)(2,1)} async-done(((bf16[768,128]{1,0:T(8,128)(2,1)}), bf16[384,128]{1,0:T(8,128)(2,1)}) %reduce-scatter.46.cloned.1.call-update) | async-done | bytes 98320
  186.6 44.2 %all-gather.14.cloned.1.call-done = bf16[4096,384]{0,1:T(8,128)(2,1)} async-done(((bf16[128,384]{0,1:T(8,128)(2,1)}), bf16[4096,384]{0,1:T(8,128)(2,1)}) %all-gather.14.cloned.1.call-update) | async-done | bytes 3145744 | tf_op jit(solution)/shard_map/all_gather | solution.py:116
  243.8 34.3 %all-gather.20.cloned.1.call-done = bf16[1,4096,384]{2,1,0:T(8,128)(2,1)} async-done(((bf16[1,128,384]{2,1,0:T(8,128)(2,1)}), bf16[1,4096,384]{2,1,0:T(8,128)(2,1)}) %all-gather.20.cloned.1.call-update) | async-done | bytes 3145744 | tf_op jit(solution)/shard_map/all_gather | solution.py:117
  295.8 14.0 %reduce-scatter.52.cloned.1.call-done = bf16[384,128]{1,0:T(8,128)(2,1)} async-done(((bf16[768,128]{1,0:T(8,128)(2,1)}), bf16[384,128]{1,0:T(8,128)(2,1)}) %reduce-scatter.52.cloned.1.call-update) | async-done | bytes 98320
  349.2 39.5 %all-gather.16.cloned.1.call-done = bf16[4096,384]{0,1:T(8,128)(2,1)} async-done(((bf16[128,384]{0,1:T(8,128)(2,1)}), bf16[4096,384]{0,1:T(8,128)(2,1)}) %all-gather.16.cloned.1.call-update) | async-done | bytes 3145744 | tf_op jit(solution)/shard_map/all_gather | solution.py:116
  398.6 37.4 %all-gather.22.cloned.1.call-done = bf16[1,4096,384]{2,1,0:T(8,128)(2,1)} async-done(((bf16[1,128,384]{2,1,0:T(8,128)(2,1)}), bf16[1,4096,384]{2,1,0:T(8,128)(2,1)}) %all-gather.22.cloned.1.call-update) | async-done | bytes 3145744 | tf_op jit(solution)/shard_map/all_gather | solution.py:117
  500.2 9.9 fusion.30
  529.8 48.3 %reduce-scatter.48.cloned.1.call-done = bf16[128,384]{1,0:T(8,128)(2,1)} async-done(((bf16[4096,384]{1,0:T(8,128)(2,1)}), bf16[128,384]{1,0:T(8,128)(2,1)}) %reduce-scatter.48.cloned.1.call-update) | async-done | bytes 98320
  588.5 73.9 %reduce-scatter.40.cloned.1.call-done = bf16[128,384]{1,0:T(8,128)(2,1)} async-done(((bf16[4096,384]{1,0:T(8,128)(2,1)}), bf16[128,384]{1,0:T(8,128)(2,1)}) %reduce-scatter.40.cloned.1.call-update) | async-done | bytes 98320 | tf_op jit(solution)/shard_map/reduce_scatter | solution.py:187
  669.1 15.9 %reduce-scatter.50.cloned.1.call-done = bf16[384,128]{1,0:T(8,128)(2,1)} async-done(((bf16[768,128]{1,0:T(8,128)(2,1)}), bf16[384,128]{1,0:T(8,128)(2,1)}) %reduce-scatter.50.cloned.1.call-update) | async-done | bytes 98320
  769.7 49.0 %reduce-scatter.54.cloned.1.call-done = bf16[128,384]{1,0:T(8,128)(2,1)} async-done(((bf16[4096,384]{1,0:T(8,128)(2,1)}), bf16[128,384]{1,0:T(8,128)(2,1)}) %reduce-scatter.54.cloned.1.call-update) | async-done | bytes 98320
  829.0 74.0 %reduce-scatter.42.cloned.1.call-done = bf16[128,384]{1,0:T(8,128)(2,1)} async-done(((bf16[4096,384]{1,0:T(8,128)(2,1)}), bf16[128,384]{1,0:T(8,128)(2,1)}) %reduce-scatter.42.cloned.1.call-update) | async-done | bytes 98320 | tf_op jit(solution)/shard_map/reduce_scatter | solution.py:187
  909.7 15.9 %reduce-scatter.56.cloned.1.call-done = bf16[384,128]{1,0:T(8,128)(2,1)} async-done(((bf16[768,128]{1,0:T(8,128)(2,1)}), bf16[384,128]{1,0:T(8,128)(2,1)}) %reduce-scatter.56.cloned.1.call-update) | async-done | bytes 98320
  978.0 9.9 fusion.36
  1044.5 15.0 %reduce-scatter.58.cloned.1.call-done = bf16[128,384]{1,0:T(8,128)(2,1)} async-done(((bf16[4096,384]{1,0:T(8,128)(2,1)}), bf16[128,384]{1,0:T(8,128)(2,1)}) %reduce-scatter.58.cloned.1.call-update) | async-done | bytes 98320
  1061.7 81.6 %reduce-scatter.44.cloned.1.call-done = bf16[128,384]{1,0:T(8,128)(2,1)} async-done(((bf16[4096,384]{1,0:T(8,128)(2,1)}), bf16[128,384]{1,0:T(8,128)(2,1)}) %reduce-scatter.44.cloned.1.call-update) | async-done | bytes 98320 | tf_op jit(solution)/shard_map/reduce_scatter | solution.py:187
  1162.5 15.6 %reduce-scatter.64.cloned.1.call-done = bf16[384,4]{1,0:T(8,128)(2,1)} async-done(((bf16[768,4]{1,0:T(8,128)(2,1)}), bf16[384,4]{1,0:T(8,128)(2,1)}) %reduce-scatter.64.cloned.1.call-update) | async-done | bytes 3088
  1180.0 14.8 %reduce-scatter.66.cloned.1.call-done = bf16[384,4]{1,0:T(8,128)(2,1)} async-done(((bf16[768,4]{1,0:T(8,128)(2,1)}), bf16[384,4]{1,0:T(8,128)(2,1)}) %reduce-scatter.66.cloned.1.call-update) | async-done | bytes 3088
  1197.3 14.1 %reduce-scatter.68.cloned.1.call-done = bf16[384,4]{1,0:T(8,128)(2,1)} async-done(((bf16[768,4]{1,0:T(8,128)(2,1)}), bf16[384,4]{1,0:T(8,128)(2,1)}) %reduce-scatter.68.cloned.1.call-update) | async-done | bytes 3088
  1212.4 124.4 %all-reduce.18 = (bf16[4,384]{1,0:T(4,128)(2,1)S(1)}, bf16[1,3,384]{2,0,1:T(2,128)(2,1)S(1)}, bf16[1,384]{1,0:T(2,128)(2,1)S(1)}, bf16[1,1536]{1,0:T(2,128)(2,1)S(1)}) all-reduce(bf16[4,384]{1,0:T(4,128)(2,1)S(1)} %add_convert_fusion.19, ...), channel_id=1, replica_groups=mesh['pipe'=2,'tensor'=2,'ctx'=32] {'ctx'}, use_global_device_ids=true, to_apply=%region_54.55 | all-reduce | flops 4608 | bytes 18432 | tf_op jit(solution)/shard_map/psum | solution.py:283
  1341.0 10.6 all-reduce.22.cloned.1.call-done
  (640 shorter events, 507.5 us)
Async XLA Ops:
  7.2 69.3 %all-gather.12.cloned.1.call-start = ((), (), s32[]{:S(2)}) async-start(), calls=%async_computation.15 | async-start | bytes 3244032 | tf_op jit(solution)/shard_map/all_gather | solution.py:116
  25.4 98.6 %all-gather.18.cloned.1.call-start = ((), (), s32[]{:S(2)}) async-start(), calls=%async_computation.21 | async-start | bytes 3244032 | tf_op jit(solution)/shard_map/all_gather | solution.py:117
  26.1 129.6 %reduce-scatter.46.cloned.1.call-start = ((), (), s32[]{:S(2)}) async-start(), calls=%async_computation.24 | async-start | bytes 294912
  141.7 89.1 %all-gather.14.cloned.1.call-start = ((), (), s32[]{:S(2)}) async-start(), calls=%async_computation.16 | async-start | bytes 3244032 | tf_op jit(solution)/shard_map/all_gather | solution.py:116
  180.0 98.1 %all-gather.20.cloned.1.call-start = ((), (), s32[]{:S(2)}) async-start(), calls=%async_computation.22 | async-start | bytes 3244032 | tf_op jit(solution)/shard_map/all_gather | solution.py:117
  181.7 128.1 %reduce-scatter.52.cloned.1.call-start = ((), (), s32[]{:S(2)}) async-start(), calls=%async_computation.27 | async-start | bytes 294912
  295.8 92.9 %all-gather.16.cloned.1.call-start = ((), (), s32[]{:S(2)}) async-start(), calls=%async_computation.18 | async-start | bytes 3244032 | tf_op jit(solution)/shard_map/all_gather | solution.py:116
  337.8 98.2 %all-gather.22.cloned.1.call-start = ((), (), s32[]{:S(2)}) async-start(), calls=%async_computation.23 | async-start | bytes 3244032 | tf_op jit(solution)/shard_map/all_gather | solution.py:117
  339.5 238.7 %reduce-scatter.48.cloned.1.call-start = ((), (), s32[]{:S(2)}) async-start(), calls=%async_computation.25 | async-start | bytes 3244032
  500.2 162.2 %reduce-scatter.40.cloned.1.call-start = ((), (), s32[]{:S(2)}) async-start(), calls=%async_computation.17 | async-start | bytes 3244032 | tf_op jit(solution)/shard_map/reduce_scatter | solution.py:187
  514.8 170.2 %reduce-scatter.50.cloned.1.call-start = ((), (), s32[]{:S(2)}) async-start(), calls=%async_computation.26 | async-start | bytes 294912
  669.0 149.6 %reduce-scatter.54.cloned.1.call-start = ((), (), s32[]{:S(2)}) async-start(), calls=%async_computation.28 | async-start | bytes 3244032
  688.3 16.1 %collective-permute-start.1 = (bf16[128,384]{1,0:T(8,128)(2,1)}, bf16[128,384]{1,0:T(8,128)(2,1)}, u32[]{:S(2)}, u32[]{:S(2)}) collective-permute-start(bf16[128,384]{1,0:T(8,128)(2,1)} %fusion.281), channel_id=1, source_target_pairs={{64,0},{65,1},{66,2},{67,3},{68,4},{69,5},{70,6},{71,7},{72,8},{73... | collective-permute-start | bytes 294920 | tf_op jit(solution)/shard_map/ppermute | solution.py:16
  736.8 166.2 %reduce-scatter.42.cloned.1.call-start = ((), (), s32[]{:S(2)}) async-start(), calls=%async_computation.19 | async-start | bytes 3244032 | tf_op jit(solution)/shard_map/reduce_scatter | solution.py:187
  751.6 174.0 %reduce-scatter.56.cloned.1.call-start = ((), (), s32[]{:S(2)}) async-start(), calls=%async_computation.29 | async-start | bytes 294912
  909.7 149.9 %reduce-scatter.58.cloned.1.call-start = ((), (), s32[]{:S(2)}) async-start(), calls=%async_computation.30 | async-start | bytes 3244032
  928.9 16.5 %collective-permute-start.3 = (bf16[128,384]{1,0:T(8,128)(2,1)}, bf16[128,384]{1,0:T(8,128)(2,1)}, u32[]{:S(2)}, u32[]{:S(2)}) collective-permute-start(bf16[128,384]{1,0:T(8,128)(2,1)} %get-tuple-element.89), channel_id=1, source_target_pairs={{64,0},{65,1},{66,2},{67,3},{68,4},{69,5},{70,6},{71,7},{72,8},{73... | collective-permute-start | bytes 294920 | tf_op jit(solution)/shard_map/ppermute | solution.py:16
  977.9 165.4 %reduce-scatter.44.cloned.1.call-start = ((), (), s32[]{:S(2)}) async-start(), calls=%async_computation.20 | async-start | bytes 3244032 | tf_op jit(solution)/shard_map/reduce_scatter | solution.py:187
  992.8 168.6 %reduce-scatter.62.cloned.1.call-start = ((), (), s32[]{:S(2)}) async-start(), calls=%async_computation.32 | async-start | bytes 294912
  1006.1 171.9 %reduce-scatter.64.cloned.1.call-start = ((), (), s32[]{:S(2)}) async-start(), calls=%async_computation.33 | async-start | bytes 294912
  1010.8 184.0 %reduce-scatter.66.cloned.1.call-start = ((), (), s32[]{:S(2)}) async-start(), calls=%async_computation.34 | async-start | bytes 294912
  1021.8 189.6 %reduce-scatter.68.cloned.1.call-start = ((), (), s32[]{:S(2)}) async-start(), calls=%async_computation.35 | async-start | bytes 294912
  1147.3 191.8 %reduce-scatter.60.cloned.1.call-start = ((), (), s32[]{:S(2)}) async-start(), calls=%async_computation.31 | async-start | bytes 294912
  1149.4 202.2 %all-reduce.22.cloned.1.call-start = ((), (), s32[]{:S(2)}) async-start(), calls=%async_computation.36 | async-start | bytes 14155776 | tf_op jit(solution)/shard_map/psum | solution.py:283
  (172 other events, 3256.1 us)
Sparse Core Ops, SparseCore 0:
  25.5 51.0 all-gather.11
  79.3 44.5 all-gather.17
  141.8 13.8 reduce-scatter.45
  180.1 50.6 all-gather.13
  233.5 44.5 all-gather.19
  295.9 13.8 reduce-scatter.51
  337.9 50.6 all-gather.15
  391.5 44.5 all-gather.21
  500.3 77.7 reduce-scatter.47
  582.6 79.7 reduce-scatter.39
  669.2 15.8 reduce-scatter.49
  737.0 81.6 reduce-scatter.53
  823.3 79.6 reduce-scatter.41
  909.8 15.7 reduce-scatter.55
  978.0 81.4 reduce-scatter.57
  1063.5 79.7 reduce-scatter.43
  1145.5 15.8 reduce-scatter.61
  1163.6 14.4 reduce-scatter.63
  1180.3 14.3 reduce-scatter.65
  1197.0 14.3 reduce-scatter.67
  1214.3 14.3 reduce-scatter.59
  1233.8 117.7 all-reduce.21
where the time goes:
time: 1380 us; the launch traced here: 1370 us
  waiting for transfers between devices  704 us (51%)
  matrix products  240 us (17%)
  blocking collectives  160 us (12%)
  local copies, waits for them, and re-layouts  155 us (11%)
  other arithmetic  86.3 us (6%)
  between operations  16.7 us (1%)
    reduce_scatter x3, waiting for transfers between devices, layer_backward(): lax.psum_scatter(value_full.astype(jnp.bfloat16), 'ctx', scatter_dimensio...  230 us
    unnamed x34, waiting for transfers between devices  225 us
    all_gather x3, waiting for transfers between devices, layer_forward(): lax.all_gather(keys, 'ctx', axis=0, tiled=True)  129 us
    psum x1, blocking collectives, body(): lax.psum(as_sent(totals), 'ctx')  124 us
    all_gather x3, waiting for transfers between devices, layer_forward(): lax.all_gather(values, 'ctx', axis=0, tiled=True)  107 us
    unnamed x365, local copies, waits for them, and re-layouts  66.4 us
    dot_general x6, matrix products, masked_scores(): jnp.einsum('chd,shd->hcs', query_heads, key_heads, preferred_element_type...  37.5 us
    dot_general x3, matrix products, attend_back(): jnp.einsum('hcs,chd->shd', probs.astype(jnp.bfloat16), grad_heads, prefer...  29.6 us
  transfers between devices with their start and end apart: 26, of which 23 were waited for; matrix products, arithmetic and copies ran while one was open for 17% of the time, Pallas kernels for 0%

commit v1 on v0

v1 whole, which is shorter than its diff:
```python
import functools

import jax
import jax.numpy as jnp
from jax import lax
from jax.experimental import pallas as pl
from jax.experimental.pallas import tpu as pltpu
from jax.sharding import PartitionSpec as P


D = 768
HD = 64
F32 = jnp.float32
BF = jnp.bfloat16
MESH = pl.DeviceIdType.MESH
EPS = 1e-05
CHIPS = 16
ROWS = 256
PIECE = 144
SLAB = CHIPS * PIECE
KV0, Q0, O0, I0, U0 = 0, 384, 576, 768, 1536
BLOCKS = ((1, 0), (2, 0), (2, 1), (1, 1), (1, 2), (2, 2), (0, 0), (0, 1), (0, 2))
NN = (((1,), (0,)), ((), ()))
NT = (((1,), (1,)), ((), ()))
TN = (((0,), (0,)), ((), ()))


def dot(a, b, dims=NN):
    return lax.dot_general(a, b, dims, preferred_element_type=F32)


class Place:
    def __init__(self):
        self.pipe = lax.axis_index("pipe")
        self.tensor = lax.axis_index("tensor")
        ctx = lax.axis_index("ctx")
        self.core = lax.rem(ctx, 2)
        self.chip = ctx // 2
        self.x = self.chip // 4
        self.z = lax.rem(self.chip, 4)

    def slot(self, dx, dz):
        return lax.rem(self.x + (dx + 4), 4) * 4 + lax.rem(self.z + (dz + 4), 4)

    def at(self, dx, dz):
        return (self.pipe, self.tensor, self.slot(dx, dz) * 2 + self.core)

    def mate(self, r):
        t = lax.rem(self.tensor + r // 2, 2)
        c = lax.rem(self.core + r % 2, 2)
        return t, c, (self.pipe, t, self.chip * 2 + c)

    def partner(self):
        return (1 - self.pipe, self.tensor, self.chip * 2 + self.core)

    def greet(self, mates=(), partner=False, far=False):
        bar = pltpu.get_barrier_semaphore()
        targets = [self.at(1, 0), self.at(-1, 0), self.at(0, 1), self.at(0, -1)]
        if far:
            targets += [self.at(2, 0), self.at(0, 2)]
        targets += [self.mate(r)[2] for r in mates]
        if partner:
            targets.append(self.partner())
        for target in targets:
            pl.semaphore_signal(bar, inc=1, device_id=target, device_id_type=MESH)
        pl.semaphore_wait(bar, len(targets))


class Links:
    def __init__(self, send_sems, recv_sems):
        self.send_sems, self.recv_sems = send_sems, recv_sems
        self.ids, self.sent = {}, []

    def desc(self, key, src, dst, device):
        i = self.ids.setdefault(key, len(self.ids))
        return pltpu.make_async_remote_copy(
            src_ref=src,
            dst_ref=dst,
            send_sem=self.send_sems.at[i],
            recv_sem=self.recv_sems.at[i],
            device_id=device,
            device_id_type=MESH,
        )

    def send(self, key, copy):
        self.desc(key, *copy()).start()
        self.sent.append((key, copy))

    def arrived(self, key, dst, device):
        self.desc(key, dst, dst, device).wait_recv()

    def finish(self):
        for key, copy in self.sent:
            self.desc(key, *copy()).wait_send()


def kv_view(h, part):
    start, size = {"all": (0, 128), 0: (0, 64), 1: (64, 64)}[part]
    return (pl.ds(h * 128 + start, size), pl.ds(0, 384))


def slab_view(h, part):
    cut = (80, 64)[h]
    start, size = {"all": (0, PIECE), 0: (0, cut), 1: (cut, PIECE - cut)}[part]
    return (pl.ds(start, size), pl.ds(h * 384, 384))


class Gather:
    def __init__(self, place, links, buf, view, tag=""):
        self.place, self.links, self.buf, self.view, self.tag = place, links, buf, view, tag

    def ref(self, du, dv, h, part):
        slot = self.place.slot(du, dv) if h == 0 else self.place.slot(dv, du)
        return self.buf.at[(slot,) + self.view(h, part)]

    def dev(self, along_u, step, h):
        return self.place.at(step, 0) if along_u == (h == 0) else self.place.at(0, step)

    def snd(self, h, along_u, step, du, dv, part):
        key = (self.tag, h, along_u, step, du - (step if along_u else 0), dv - (0 if along_u else step), part)
        ref = lambda: self.ref(du, dv, h, part)
        self.links.send(key, lambda: (ref(), ref(), self.dev(along_u, step, h)))

    def rcv(self, h, along_u, step, du, dv, part):
        key = (self.tag, h, along_u, step, du, dv, part)
        self.links.arrived(key, self.ref(du, dv, h, part), self.dev(along_u, step, h))

    def begin(self):
        for along_u in (True, False):
            for h in (0, 1):
                for step in (1, -1):
                    self.snd(h, along_u, step, 0, 0, "all")

    def first(self):
        for h in (0, 1):
            for step, part in ((1, 0), (-1, 1)):
                self.rcv(h, True, step, -step, 0, "all")
                self.snd(h, True, step, -step, 0, part)
                for s in (1, -1):
                    self.snd(h, False, s, -step, 0, "all")

    def second(self):
        for h in (0, 1):
            for step, part in ((1, 0), (-1, 1)):
                self.rcv(h, True, step, -2 * step, 0, part)
            for s in (1, -1):
                self.snd(h, False, s, 2, 0, "all")

    def third(self, du):
        for h in (0, 1):
            for step, part in ((1, 0), (-1, 1)):
                self.rcv(h, False, step, du, -step, "all")
                self.snd(h, False, step, du, -step, part)

    def fourth(self, du):
        for h in (0, 1):
            for step, part in ((1, 0), (-1, 1)):
                self.rcv(h, False, step, du, -2 * step, part)

    def run(self, done=lambda a, b: None):
        self.begin()
        done(0, 0)
        self.first()
        self.second()
        for stage, du, slots in (
            (self.third, 0, ORDER_F[0:4]),
            (self.third, -1, ORDER_F[4:5]),
            (self.third, 1, ORDER_F[5:8]),
            (self.third, 2, ()),
            (self.fourth, 0, ORDER_F[8:10]),
            (self.fourth, -1, ORDER_F[10:12]),
            (self.fourth, 1, ORDER_F[12:14]),
            (self.fourth, 2, ORDER_F[14:15]),
        ):
            stage(du)
            for a, b in slots:
                done(a, b)


class Scatter:
    def __init__(self, place, links, buf, view, r1, r2, u1, u2, tag=""):
        self.place, self.links, self.buf, self.view = place, links, buf, view
        self.r1, self.r2, self.u1, self.u2, self.tag = r1, r2, u1, u2, tag

    def ref(self, du, dv, h, part):
        slot = self.place.slot(du, dv) if h == 0 else self.place.slot(dv, du)
        return self.buf.at[(slot,) + self.view(h, part)]

    def dev(self, along_u, step, h):
        return self.place.at(step, 0) if along_u == (h == 0) else self.place.at(0, step)

    def size(self, h, part):
        return pl.ds(0, self.view(h, part)[0].size)

    def land(self, stage, h, step, du):
        d, e = (step + 1) // 2, (du + 4) % 4
        part = (1 - d) if stage in ("v1", "u1") else "all"
        rows = self.size(h, part)
        return {
            "v1": lambda: self.r1.at[h, d, e, rows],
            "v2": lambda: self.r2.at[h, d, e, rows],
            "u1": lambda: self.u1.at[h, d, rows],
            "u2": lambda: self.u2.at[h, d, rows],
        }[stage]()

    def snd(self, stage, h, step, du, src):
        key = (self.tag, stage, h, step, du)
        device = lambda: self.dev(stage[0] == "u", step, h)
        self.links.send(key, lambda: (src(), self.land(stage, h, step, du), device()))

    def rcv(self, stage, h, step, du):
        ref = self.land(stage, h, step, du)
        self.links.arrived((self.tag, stage, h, step, du), ref, self.dev(stage[0] == "u", step, h))
        return ref

    def v1(self, h, step, du):
        self.snd("v1", h, step, du, lambda: self.ref(du, 2, h, (1 - step) // 2))

    def v2(self, h, step, du):
        got = self.rcv("v1", h, step, du)
        mine = self.ref(du, step, h, (1 - step) // 2)
        mine[...] = (mine[...].astype(F32) + got[...].astype(F32)).astype(BF)
        self.snd("v2", h, step, du, lambda: self.ref(du, step, h, "all"))

    def vsum(self, h, du):
        one, two = self.rcv("v2", h, 1, du), self.rcv("v2", h, -1, du)
        mine = self.ref(du, 0, h, "all")
        mine[...] = (mine[...].astype(F32) + one[...].astype(F32) + two[...].astype(F32)).astype(BF)

    def u1s(self, h):
        for step in (1, -1):
            self.snd("u1", h, step, 0, lambda step=step: self.ref(2, 0, h, (1 - step) // 2))

    def u2s(self, h, step):
        got = self.rcv("u1", h, step, 0)
        mine = self.ref(step, 0, h, (1 - step) // 2)
        mine[...] = (mine[...].astype(F32) + got[...].astype(F32)).astype(BF)
        self.snd("u2", h, step, 0, lambda: self.ref(step, 0, h, "all"))

    def last(self, h):
        one, two = self.rcv("u2", h, 1, 0), self.rcv("u2", h, -1, 0)
        mine = self.ref(0, 0, h, "all")
        return mine[...].astype(F32) + one[...].astype(F32) + two[...].astype(F32)

    def tail_one(self):
        for h in (0, 1):
            self.vsum(h, 2)
            self.u1s(h)

    def tail_two(self):
        for h in (0, 1):
            for step in (1, -1):
                self.vsum(h, step)
                self.u2s(h, step)

    def tail_three(self):
        for h in (0, 1):
            self.vsum(h, 0)


def pick(n, values):
    out = 0
    for j, v in enumerate(values):
        out = out + (n == j).astype(jnp.int32) * v
    return out


def mates_gather(place, links, own, full, tag):
    rows = pl.ds(pl.multiple_of(place.core * 128, 128), 128)
    for r in (1, 2, 3):
        device = place.mate(r)[2]
        links.send((tag, r), lambda device=device: (own, full.at[place.tensor, rows], device))
    full[place.tensor, rows] = own[...]


def mates_gathered(place, links, full, tag):
    for r in (1, 2, 3):
        t, c, device = place.mate(r)
        links.arrived((tag, r), full.at[t, pl.ds(pl.multiple_of(c * 128, 128), 128)], device)


def mates_scatter(place, links, part, rounded, landing, tag):
    rounded[...] = part[...].astype(BF)
    for r in (1, 2, 3):
        t, c, device = place.mate(r)
        src = rounded.at[t, pl.ds(pl.multiple_of(c * 128, 128), 128)]
        links.send((tag, r), lambda r=r, src=src, device=device: (src, landing.at[r - 1], device))


def mates_scattered(place, links, part, landing, tag):
    total = part[place.tensor, pl.ds(pl.multiple_of(place.core * 128, 128), 128)]
    for r in (1, 2, 3):
        links.arrived((tag, r), landing.at[r - 1], place.mate(r)[2])
        total = total + landing[r - 1].astype(F32)
    return total


def normalize(values):
    centered = values - jnp.mean(values, axis=-1, keepdims=True)
    variance = jnp.mean(centered * centered, axis=-1, keepdims=True)
    scale = lax.rsqrt(variance + EPS)
    return centered * scale, scale


def lane_mask(lower, shape=(ROWS, 128)):
    lane = lax.broadcasted_iota(jnp.int32, shape, 1)
    return lane < 64 if lower else lane >= 64


def turn(values, tab, lower, upper, sign=1.0):
    cosine, plus, minus = tab[0], tab[1], tab[2]
    turned = (
        values * cosine
        + sign * (pltpu.roll(values, 8, 1) * plus + pltpu.roll(values, 120, 1) * minus)
    )
    if lower and upper:
        return turned
    return jnp.where(lane_mask(lower), turned, values)


def weights_kernel(
    qkv, out, fc_in, fc_out, gain, shift, qkv_b, in_b, out_b, mine, theirs, all_small,
    own, buf, raw, turned, small, got_small, send_sems, recv_sems, local,
):
    place = Place()
    links = Links(send_sems, recv_sems)
    core = place.core
    loads = [pltpu.make_async_copy(qkv, raw, local.at[0])]
    for i, block in enumerate((1, 0, 2)):
        rows = pl.ds(pl.multiple_of(core * 192 + block * 64, 64), 64)
        loads.append(pltpu.make_async_copy(out.at[rows], own.at[pl.ds(O0 + i * 64, 64)], local.at[1 + i]))
    half = pl.ds(pl.multiple_of(core * 768, 768), 768)
    loads.append(pltpu.make_async_copy(fc_in.at[:, half], own.at[pl.ds(I0, 768)], local.at[4]))
    loads.append(pltpu.make_async_copy(fc_out.at[half], own.at[pl.ds(U0, 768)], local.at[5]))
    for load in loads:
        load.start()
    place.greet(partner=True)
    small[...] = jnp.zeros_like(small)
    small[0:2] = gain[...].astype(F32)
    small[2:4] = shift[...].astype(F32)
    bias = qkv_b[...].astype(F32)
    bias = jnp.where(core == 0, bias[:, 0:192], bias[:, 192:384])
    pieces = [bias[j : j + 1, h * 64 : h * 64 + 64] for j, h in BLOCKS]
    small[4:5, 0:576] = jnp.concatenate(pieces, axis=1)
    wide = in_b[...].astype(F32)
    small[5:6] = jnp.where(core == 0, wide[:, 0:768], wide[:, 768:1536])
    small[6:7, 0:384] = out_b[...].astype(F32)
    rounded = small[...].astype(BF)
    all_small[place.pipe] = rounded
    loads[0].wait()
    for j in range(3):
        turned[...] = raw[j].T
        for i, (k, h) in enumerate(BLOCKS):
            if k == j:
                own[i * 64 : i * 64 + 64, :] = turned[pl.ds(pl.multiple_of(core * 192 + h * 64, 64), 64), :]
    for load in loads[1:]:
        load.wait()
    device = place.partner()
    piece = pl.ds(pl.multiple_of(place.chip * PIECE, PIECE), PIECE)
    links.send("slab", lambda: (own.at[piece], buf.at[place.chip], device))
    got_small[0] = rounded
    links.send("small", lambda: (got_small.at[0], got_small.at[1], device))
    keep = pltpu.make_async_copy(own, mine, local.at[6])
    keep.start()
    links.arrived("slab", buf.at[place.chip], device)
    Gather(place, links, buf, slab_view).run()
    store = pltpu.make_async_copy(buf, theirs, local.at[7])
    store.start()
    links.arrived("small", got_small.at[1], device)
    all_small[1 - place.pipe] = got_small[1]
    keep.wait()
    store.wait()
    links.finish()


def load_layer(l, place, mine, theirs, w, sem):
    pl.when(place.pipe == l)(lambda: pltpu.make_async_copy(mine, w, sem).start())
    pl.when(place.pipe != l)(lambda: pltpu.make_async_copy(theirs, w, sem).start())
    return pltpu.make_async_copy(mine, w, sem)


ORDER_F = ((0, -1), (0, 1), (-1, 0), (1, 0), (-1, -1), (-1, 1), (1, -1), (1, 1), (0, 2), (2, 0), (-1, 2), (2, -1), (1, 2), (2, 1), (2, 2))
ORDER_B = ((2, 2), (0, 2), (2, 0), (-1, 2), (1, 2), (2, -1), (2, 1), (-1, -1), (-1, 1), (1, -1), (1, 1), (0, -1), (0, 1), (-1, 0), (1, 0))


def forward_kernel(
    l, x_ref, slab, slab2, small, tab, y_ref, xg_o, kv_o, q_o, ot_o, lse_o, inner_o,
    w, xg, kvb, acc, top, total, part, rounded, landing, send_sems, recv_sems, local,
):
    place = Place()
    links = Links(send_sems, recv_sems)
    load = load_layer(l, place, slab, slab2, w, local.at[0])
    place.greet(mates=(1, 2, 3))
    mates_gather(place, links, x_ref, xg, "x")
    vectors = small[l].astype(F32)
    mates_gathered(place, links, xg, "x")
    xg_o[...] = xg[...]
    x = jnp.concatenate([xg[0], xg[1]], axis=1).astype(F32)
    normed, _ = normalize(x)
    first = (normed * vectors[0:1] + vectors[2:3]).astype(BF)
    second = (normed * vectors[1:2] + vectors[3:4]).astype(BF)
    load.wait()
    kv = dot(first, w[KV0:Q0, :], NT) + vectors[4:5, 0:384]
    for h in range(3):
        tile = kv[:, h * 128 : h * 128 + 128]
        kvb[place.chip, :, h * 128 : h * 128 + 128] = turn(tile, tab, h != 1, h == 1).astype(BF)
    gather = Gather(place, links, kvb, kv_view)
    gather.begin()
    low, high = lane_mask(True), lane_mask(False)
    qa = dot(first, w[Q0 : Q0 + 128, :], NT) + vectors[4:5, 384:512]
    qb = dot(first, w[Q0 + 64 : Q0 + 192, :], NT)
    qa = (turn(qa, tab, True, True)).astype(BF) * HD**-0.5
    qb = pltpu.roll(qb, 64, 1) + vectors[4:5, 512:640]
    qb = (turn(qb, tab, True, False)).astype(BF) * HD**-0.5
    zero = jnp.zeros((ROWS, 128), BF)
    q_o[0] = jnp.where(low, qa, zero)
    q_o[1] = jnp.where(high, qa, zero)
    q_o[2] = jnp.where(low, qb, zero)
    gather.first()
    inner = dot(second, w[I0:U0, :]) + vectors[5:6]
    inner_o[...] = inner
    act = (inner * (0.5 * (1.0 + lax.erf(inner * (2.0**-0.5))))).astype(BF)
    gather.second()
    branch = dot(act, w[U0:SLAB, :])
    part[0] = branch[:, 0:384]
    part[1] = branch[:, 384:768]

    def scores(kk, h):
        keys = kvb[kk, :, h * 128 : h * 128 + 128]
        return keys, dot(keys, q_o[h], NT)

    causal = lax.broadcasted_iota(jnp.int32, (ROWS, ROWS), 0) <= lax.broadcasted_iota(
        jnp.int32, (ROWS, ROWS), 1
    )
    for h in range(3):
        keys, s = scores(place.chip, h)
        s = jnp.where(causal, s, -1e30)
        m = jnp.max(s, axis=0, keepdims=True)
        p = jnp.exp(s - m)
        top[h] = m
        total[h] = jnp.sum(p, axis=0, keepdims=True)
        acc[h] = dot(keys, p.astype(BF), TN)

    def step(n, carry):
        for j, action in (
            (0, lambda: gather.third(0)),
            (4, lambda: gather.third(-1)),
            (5, lambda: gather.third(1)),
            (8, lambda: gather.fourth(0)),
            (9, lambda: gather.third(2)),
            (10, lambda: gather.fourth(-1)),
            (12, lambda: gather.fourth(1)),
            (14, lambda: gather.fourth(2)),
        ):
            pl.when(n == j)(action)
        kk = place.slot(pick(n, [o[0] for o in ORDER_F]), pick(n, [o[1] for o in ORDER_F]))

        @pl.when(kk < place.chip)
        def _():
            for h in range(3):
                keys, s = scores(kk, h)
                old = top[h]
                m = jnp.maximum(old, jnp.max(s, axis=0, keepdims=True))
                p = jnp.exp(s - m)
                fade = jnp.exp(old - m)
                top[h] = m
                total[h] = total[h] * fade + jnp.sum(p, axis=0, keepdims=True)
                acc[h] = acc[h] * fade + dot(keys, p.astype(BF), TN)

        return carry

    lax.fori_loop(0, 15, step, 0)
    store = pltpu.make_async_copy(kvb, kv_o, local.at[1])
    store.start()
    heads = []
    for h in range(3):
        rows = slice(0, 64) if h == 1 else slice(64, 128)
        heads.append(acc[h, rows, :] / total[h])
        lse_o[h : h + 1, :] = top[h] + jnp.log(total[h])
    attn = jnp.concatenate([heads[1], heads[0], heads[2]], axis=0)
    ot_o[...] = attn
    branch = dot(attn.astype(BF), w[O0:I0, :], TN)
    part[0] = part[0] + branch[:, 0:384]
    part[1] = part[1] + branch[:, 384:768]
    mates_scatter(place, links, part, rounded, landing, "y")
    y = mates_scattered(place, links, part, landing, "y")
    y_ref[...] = (y + x_ref[...].astype(F32) + vectors[6:7, 0:384]).astype(BF)
    store.wait()
    links.finish()


def backward_kernel(
    l, g_ref, xg, slab, slab2, small, tab, tabt, kv, q, ot, lse, inner, gx_ref, wg, sg,
    w, gg, kvb, dkv, dqt, do, first, second, act, slope, part, rounded, landing,
    r1, r2, u1, u2, send_sems, recv_sems, local,
):
    place = Place()
    links = Links(send_sems, recv_sems)
    load = load_layer(l, place, slab, slab2, w, local.at[0])
    load_kv = pltpu.make_async_copy(kv, kvb, local.at[1])
    load_kv.start()
    place.greet(mates=(1, 2, 3))
    mates_gather(place, links, g_ref, gg, "g")
    vectors = small[l].astype(F32)
    x = jnp.concatenate([xg[0], xg[1]], axis=1).astype(F32)
    normed, scale = normalize(x)
    first[...] = (normed * vectors[0:1] + vectors[2:3]).astype(BF)
    second[...] = (normed * vectors[1:2] + vectors[3:4]).astype(BF)
    value = inner[...]
    cdf = 0.5 * (1.0 + lax.erf(value * (2.0**-0.5)))
    act[...] = (value * cdf).astype(BF)
    slope[...] = cdf + value * jnp.exp(-0.5 * value * value) * 0.3989422804014327
    load.wait()
    mates_gathered(place, links, gg, "g")
    g = jnp.concatenate([gg[0], gg[1]], axis=1)
    low, high = lane_mask(True), lane_mask(False)
    zero = jnp.zeros((ROWS, 128), BF)
    da = dot(g, w[O0 : O0 + 128, :], NT).astype(BF)
    db = dot(g, w[O0 + 64 : O0 + 192, :], NT).astype(BF)
    do[0] = jnp.where(high, da, zero)
    do[1] = jnp.where(low, da, zero)
    do[2] = jnp.where(high, db, zero)
    dot_t = dot(w[O0:I0, :], g, NT).astype(BF).astype(F32) * ot[...]
    delta = [
        jnp.sum(dot_t[s : s + 64], axis=0, keepdims=True) for s in (64, 0, 128)
    ]
    load_kv.wait()
    dqt[...] = jnp.zeros_like(dqt)
    scatter = Scatter(place, links, dkv, kv_view, r1, r2, u1, u2)

    def chunk(kk, mask):
        for h in range(3):
            keys = kvb[kk, :, h * 128 : h * 128 + 128]
            p = jnp.exp(dot(keys, q[h], NT) - lse[h : h + 1, :])
            if mask is not None:
                p = jnp.where(mask, p, 0.0)
            dp = dot(keys, do[h], NT)
            ds = (p * (dp - delta[h])).astype(BF)
            dkv[kk, :, h * 128 : h * 128 + 128] = (dot(ds, q[h]) + dot(p.astype(BF), do[h])).astype(BF)
            dqt[h] = dqt[h] + dot(keys, ds, TN)

    def events(j):
        a, b = ORDER_B[j]
        if b == 2:
            for s in (1, -1):
                scatter.v1(0, s, a)
        if a == 2:
            for s in (1, -1):
                scatter.v1(1, s, b)
        if j == 7:
            for s in (1, -1):
                scatter.v2(0, s, 2)
                scatter.v2(1, s, 2)
        if j >= 7:
            if b in (1, -1):
                scatter.v2(0, b, a)
            if a in (1, -1):
                scatter.v2(1, a, b)

    def step(n, carry):
        kk = place.slot(pick(n, [o[0] for o in ORDER_B]), pick(n, [o[1] for o in ORDER_B]))

        @pl.when(kk < place.chip)
        def _():
            chunk(kk, None)

        @pl.when(kk > place.chip)
        def _():
            dkv[kk] = jnp.zeros((ROWS, 384), BF)

        for j in range(15):
            pl.when(n == j)(functools.partial(events, j))
        return carry

    lax.fori_loop(0, 15, step, 0)
    chunk(
        place.chip,
        lax.broadcasted_iota(jnp.int32, (ROWS, ROWS), 0)
        <= lax.broadcasted_iota(jnp.int32, (ROWS, ROWS), 1),
    )
    g = jnp.concatenate([gg[0], gg[1]], axis=1)
    grad_inner = (dot(g, w[U0:SLAB, :], NT) * slope[...]).astype(BF)
    wg[U0:SLAB, :] = dot(act[...], g, TN).astype(BF)
    scatter.tail_one()
    wg[I0:U0, :] = dot(second[...], grad_inner, TN).astype(BF)
    scatter.tail_two()
    grad_second = dot(grad_inner, w[I0:U0, :], NT)
    wg[O0:I0, :] = dot(ot[...].astype(BF), g).astype(BF)
    scatter.tail_three()
    sg[0:1, :] = jnp.sum(grad_second * normed, axis=0, keepdims=True)
    sg[1:2, :] = jnp.sum(grad_second, axis=0, keepdims=True)
    sg[2:3, :] = jnp.sum(grad_inner.astype(F32), axis=0, keepdims=True)
    sg[3:4, :] = jnp.sum(g.astype(F32), axis=0, keepdims=True)
    sg[6:8, :] = jnp.zeros((2, D), F32)
    rows = []
    for h in range(3):
        base = 64 if h == 1 else 0
        dq = dqt[h, base : base + 64, :] * HD**-0.5
        a, b = dq[0:8], dq[8:16]
        rows += [a * tabt[0] + b * tabt[1], b * tabt[0] - a * tabt[1], dq[16:64]]
    dq = jnp.concatenate(rows, axis=0).astype(BF)
    wg[Q0:O0, :] = dot(dq, first[...]).astype(BF)
    grad_first = dot(dq, w[Q0:O0, :], TN)
    q_sums = dot(jnp.ones((8, ROWS), BF), dq, NT)
    pre = jnp.concatenate([scatter.last(0), scatter.last(1)], axis=0)
    tiles = [
        turn(pre[:, h * 128 : h * 128 + 128], tab, h != 1, h == 1, -1.0).astype(BF)
        for h in range(3)
    ]
    pre = jnp.concatenate(tiles, axis=1)
    wg[KV0:Q0, :] = dot(pre, first[...], TN).astype(BF)
    grad_first = grad_first + dot(pre, w[KV0:Q0, :])
    sg[4:5, :] = jnp.sum(grad_first * normed, axis=0, keepdims=True)
    sg[5:6, :] = jnp.sum(grad_first, axis=0, keepdims=True)
    sg[6:7, 0:384] = jnp.sum(pre.astype(F32), axis=0, keepdims=True)
    sg[7:8, 0:192] = q_sums[0:1, :]
    grad_norm = grad_first * vectors[0:1] + grad_second * vectors[1:2]
    grad_x = scale * (
        grad_norm
        - jnp.mean(grad_norm, axis=-1, keepdims=True)
        - normed * jnp.mean(grad_norm * normed, axis=-1, keepdims=True)
    )
    part[0] = grad_x[:, 0:384]
    part[1] = grad_x[:, 384:768]
    mates_scatter(place, links, part, rounded, landing, "gx")
    grad = mates_scattered(place, links, part, landing, "gx")
    gx_ref[...] = (grad + g_ref[...].astype(F32)).astype(BF)
    links.finish()


def grads_kernel(
    wg0, wg1, sg0, sg1, out, out_small, buf, own, other, piece, got, r1, r2, u1, u2,
    sm, along_x, along_z, across, beside, send_sems, recv_sems, local
):
    place = Place()
    links = Links(send_sems, recv_sems)
    load_theirs = load_layer(1, place, wg0, wg1, other, local.at[0])
    load_mine = load_layer(0, place, wg0, wg1, own, local.at[1])
    place.greet(mates=(1, 2, 3), partner=True, far=True)
    sm[0, 0] = sg0[...]
    sm[0, 1] = sg1[...]
    for d in (1, 2, 3):
        links.send(("sx", d), lambda d=d: (sm.at[0], along_x.at[d - 1], place.at(d, 0)))

    def small_z():
        total = sm[0]
        for d in (1, 2, 3):
            links.arrived(("sx", d), along_x.at[d - 1], place.at(d, 0))
            total = total + along_x[d - 1]
        sm[1] = total
        for d in (1, 2, 3):
            links.send(("sz", d), lambda d=d: (sm.at[1], along_z.at[d - 1], place.at(0, d)))

    def small_pipe():
        total = sm[1]
        for d in (1, 2, 3):
            links.arrived(("sz", d), along_z.at[d - 1], place.at(0, d))
            total = total + along_z[d - 1]
        sm[2] = total
        links.send("sp", lambda: (sm.at[2, 1 - place.pipe], across, place.partner()))

    def small_mates():
        links.arrived("sp", across, place.partner())
        sm[3, 0] = sm[2, place.pipe] + across[...]
        for r in (1, 2, 3):
            links.send(("sm", r), lambda r=r: (sm.at[3, 0], beside.at[r - 1], place.mate(r)[2]))

    def small_last():
        total = sm[3, 0]
        for r in (1, 2, 3):
            links.arrived(("sm", r), beside.at[r - 1], place.mate(r)[2])
            total = total + beside[r - 1]
        row = lax.broadcasted_iota(jnp.int32, (8, D), 0)
        norm = (row < 2) | ((row >= 4) & (row < 6))
        out_small[place.core] = jnp.where(norm, total, sm[3, 0])
        out_small[1 - place.core] = jnp.where(norm, total, beside[0])

    sums = []
    for i, ref in ((0, other), (1, own)):
        (load_theirs, load_mine)[i].wait()
        scatter = Scatter(place, links, ref, slab_view, r1.at[i], r2.at[i], u1.at[i], u2.at[i], i)
        sums.append(scatter)
        for du in (2, -1, 1, 0):
            for h in (0, 1):
                for s in (1, -1):
                    scatter.v1(h, s, du)
    small_z()
    for scatter in sums:
        for du in (2, -1, 1, 0):
            for h in (0, 1):
                for s in (1, -1):
                    scatter.v2(h, s, du)
    small_pipe()
    device = place.partner()
    for i, scatter in enumerate(sums):
        scatter.tail_one()
        scatter.tail_two()
        scatter.tail_three()
        for h in (0, 1):
            piece[i, :, h * 384 : h * 384 + 384] = scatter.last(h)
        if i == 0:
            got[0] = piece[0].astype(BF)
            links.send("piece", lambda: (got.at[0], got.at[1], device))
    links.arrived("piece", got.at[1], device)
    small_mates()
    buf[place.core, place.chip] = (piece[1] + got[1].astype(F32)).astype(BF)
    sibling = place.mate(1)[2]

    def pass_on(a, b):
        ref = lambda: buf.at[place.core, place.slot(a, b)]
        links.send(("core", a, b), lambda: (ref(), ref(), sibling))

    Gather(place, links, buf.at[place.core], slab_view, "g").run(pass_on)
    keep = pltpu.make_async_copy(buf.at[place.core], out.at[place.core], local.at[0])
    keep.start()
    small_last()
    for a, b in ((0, 0), *ORDER_F):
        links.arrived(("core", a, b), buf.at[1 - place.core, place.slot(a, b)], sibling)
    rest = pltpu.make_async_copy(buf.at[1 - place.core], out.at[1 - place.core], local.at[1])
    rest.start()
    keep.wait()
    rest.wait()
    links.finish()


VMEM = pl.BlockSpec(memory_space=pltpu.VMEM)
ANY = pl.BlockSpec(memory_space=pl.ANY)


def sems(n, m):
    return [pltpu.SemaphoreType.DMA((n,)), pltpu.SemaphoreType.DMA((n,)), pltpu.SemaphoreType.DMA((m,))]


def shape(dims, kind=BF):
    return jax.ShapeDtypeStruct(dims, kind)


def params(i):
    return pltpu.CompilerParams(collective_id=i, has_side_effects=True, vmem_limit_bytes=56 * 2**20)


def share_weights(*args):
    return pl.pallas_call(
        weights_kernel,
        name="share_weights",
        out_shape=(shape((SLAB, D)), shape((CHIPS, PIECE, D)), shape((2, 16, D))),
        in_specs=[ANY, ANY, ANY, ANY, VMEM, VMEM, VMEM, VMEM, VMEM],
        out_specs=(ANY, ANY, VMEM),
        scratch_shapes=[
            pltpu.VMEM((SLAB, D), BF),
            pltpu.VMEM((CHIPS, PIECE, D), BF),
            pltpu.VMEM((3, D, 384), BF),
            pltpu.VMEM((384, D), BF),
            pltpu.VMEM((16, D), F32),
            pltpu.VMEM((2, 16, D), BF),
            *sems(48, 8),
        ],
        compiler_params=params(0),
    )(*args)


def forward(l, x, slab, small, tab):
    return pl.pallas_call(
        functools.partial(forward_kernel, l),
        name=f"layer_{l}_forward",
        out_shape=(
            shape((128, 384)),
            shape((2, ROWS, 384)),
            shape((CHIPS, ROWS, 384)),
            shape((3, ROWS, 128)),
            shape((192, ROWS), F32),
            shape((8, ROWS), F32),
            shape((ROWS, D), F32),
        ),
        in_specs=[VMEM, ANY, ANY, VMEM, VMEM],
        out_specs=(VMEM, VMEM, ANY, VMEM, VMEM, VMEM, VMEM),
        scratch_shapes=[
            pltpu.VMEM((SLAB, D), BF),
            pltpu.VMEM((2, ROWS, 384), BF),
            pltpu.VMEM((CHIPS, ROWS, 384), BF),
            pltpu.VMEM((3, 128, ROWS), F32),
            pltpu.VMEM((3, 1, ROWS), F32),
            pltpu.VMEM((3, 1, ROWS), F32),
            pltpu.VMEM((2, ROWS, 384), F32),
            pltpu.VMEM((2, ROWS, 384), BF),
            pltpu.VMEM((3, 128, 384), BF),
            *sems(48, 2),
        ],
        compiler_params=params(1 + l),
    )(x, *slab, small, tab)


def landing_shapes(rows, part, lead=()):
    return [
        pltpu.VMEM((*lead, 2, 2, 4, part, 384), BF),
        pltpu.VMEM((*lead, 2, 2, 4, rows, 384), BF),
        pltpu.VMEM((*lead, 2, 2, part, 384), BF),
        pltpu.VMEM((*lead, 2, 2, rows, 384), BF),
    ]


def backward(l, g, kept, slab, small, tab, tabt):
    xg, kv, q, ot, lse, inner = kept
    return pl.pallas_call(
        functools.partial(backward_kernel, l),
        name=f"layer_{l}_backward",
        out_shape=(shape((128, 384)), shape((SLAB, D)), shape((8, D), F32)),
        in_specs=[VMEM, VMEM, ANY, ANY, VMEM, VMEM, VMEM, ANY, VMEM, VMEM, VMEM, VMEM],
        out_specs=(VMEM, VMEM, VMEM),
        scratch_shapes=[
            pltpu.VMEM((SLAB, D), BF),
            pltpu.VMEM((2, ROWS, 384), BF),
            pltpu.VMEM((CHIPS, ROWS, 384), BF),
            pltpu.VMEM((CHIPS, ROWS, 384), BF),
            pltpu.VMEM((3, 128, ROWS), F32),
            pltpu.VMEM((3, ROWS, 128), BF),
            pltpu.VMEM((ROWS, D), BF),
            pltpu.VMEM((ROWS, D), BF),
            pltpu.VMEM((ROWS, D), BF),
            pltpu.VMEM((ROWS, D), F32),
            pltpu.VMEM((2, ROWS, 384), F32),
            pltpu.VMEM((2, ROWS, 384), BF),
            pltpu.VMEM((3, 128, 384), BF),
            *landing_shapes(128, 64),
            *sems(56, 2),
        ],
        compiler_params=params(3 + l),
    )(g, xg, *slab, small, tab, tabt, kv, q, ot, lse, inner)


def share_grads(*args):
    return pl.pallas_call(
        grads_kernel,
        name="share_grads",
        out_shape=(shape((2, CHIPS, PIECE, D)), shape((2, 8, D), F32)),
        in_specs=[ANY, ANY, VMEM, VMEM],
        out_specs=(ANY, VMEM),
        scratch_shapes=[
            pltpu.VMEM((2, CHIPS, PIECE, D), BF),
            pltpu.VMEM((CHIPS, PIECE, D), BF),
            pltpu.VMEM((CHIPS, PIECE, D), BF),
            pltpu.VMEM((2, PIECE, D), F32),
            pltpu.VMEM((2, PIECE, D), BF),
            *landing_shapes(PIECE, 80, (2,)),
            pltpu.VMEM((4, 2, 8, D), F32),
            pltpu.VMEM((3, 2, 8, D), F32),
            pltpu.VMEM((3, 2, 8, D), F32),
            pltpu.VMEM((8, D), F32),
            pltpu.VMEM((3, 8, D), F32),
            *sems(160, 2),
        ],
        compiler_params=params(5),
    )(*args)


def finish_kernel(
    whole, small, g_qkv, g_out, g_in, g_down, g_gain, g_shift, g_qkv_b, g_out_b, g_in_b,
    held, qkv, out, wide, down, local,
):
    regions = ((U0, SLAB), (I0, U0), (O0, I0), (KV0, O0))
    loads = []
    for i, (lo, hi) in enumerate(regions):
        for c in (0, 1):
            rows = pl.ds(lo, hi - lo)
            load = pltpu.make_async_copy(whole.at[c, rows], held.at[c, rows], local.at[2 * i + c])
            load.start()
            loads.append(load)
    tensor = lax.axis_index("tensor")
    rows = [small[0], small[1]]

    def features(row):
        return jnp.where(tensor == 0, row[:, 0:384], row[:, 384:768])

    g_gain[0:1] = features(rows[0][4:5])
    g_gain[1:2] = features(rows[0][0:1])
    g_shift[0:1] = features(rows[0][5:6])
    g_shift[1:2] = features(rows[0][1:2])
    g_out_b[...] = features(rows[0][3:4])
    g_in_b[...] = jnp.concatenate([rows[0][2:3], rows[1][2:3]], axis=1)
    for j in range(3):
        pieces = []
        for c in (0, 1):
            for i in [BLOCKS.index((j, h)) for h in range(3)]:
                row, at = (6, i) if i < 6 else (7, i - 6)
                pieces.append(rows[c][row : row + 1, at * 64 : at * 64 + 64])
        g_qkv_b[j : j + 1] = jnp.concatenate(pieces, axis=1)
    stores = []

    def store(i, src, dst):
        copy = pltpu.make_async_copy(src, dst, local.at[8 + i])
        copy.start()
        stores.append(copy)

    for c in (0, 1):
        loads[c].wait()
        down[c * 768 : c * 768 + 768] = held[c, U0:SLAB].astype(F32)
        store(c, down.at[pl.ds(c * 768, 768)], g_down.at[pl.ds(c * 768, 768)])
    for c in (0, 1):
        loads[2 + c].wait()
        wide[:, c * 768 : c * 768 + 768] = held[c, I0:U0].astype(F32)
    store(2, wide, g_in)
    for c in (0, 1):
        loads[4 + c].wait()
        for i, block in enumerate((1, 0, 2)):
            start = c * 192 + block * 64
            out[start : start + 64] = held[c, O0 + i * 64 : O0 + i * 64 + 64].astype(F32)
    store(3, out, g_out)
    for c in (0, 1):
        loads[6 + c].wait()
    for j in range(3):
        pieces = []
        for c in (0, 1):
            for i in [BLOCKS.index((j, h)) for h in range(3)]:
                pieces.append(held[c, i * 64 : i * 64 + 64])
        qkv[j] = jnp.concatenate(pieces, axis=0).astype(F32).T
        store(4 + j, qkv.at[j], g_qkv.at[j])
    for copy in stores:
        copy.wait()


def finish(whole, small):
    return pl.pallas_call(
        finish_kernel,
        name="finish",
        out_shape=(
            shape((3, D, 384), F32),
            shape((384, D), F32),
            shape((D, 1536), F32),
            shape((1536, D), F32),
            shape((2, 384), F32),
            shape((2, 384), F32),
            shape((3, 384), F32),
            shape((1, 384), F32),
            shape((1, 1536), F32),
        ),
        in_specs=[ANY, VMEM],
        out_specs=(ANY, ANY, ANY, ANY, VMEM, VMEM, VMEM, VMEM, VMEM),
        scratch_shapes=[
            pltpu.VMEM((2, SLAB, D), BF),
            pltpu.VMEM((3, D, 384), F32),
            pltpu.VMEM((384, D), F32),
            pltpu.VMEM((D, 1536), F32),
            pltpu.VMEM((1536, D), F32),
            pltpu.SemaphoreType.DMA((16,)),
        ],
        compiler_params=pltpu.CompilerParams(vmem_limit_bytes=56 * 2**20),
    )(whole, small)


def rope_tables(chip):
    half = HD // 8
    freqs = 10000.0 ** (-2.0 * jnp.arange(half, dtype=F32) / (2 * half))
    positions = chip * ROWS + jnp.arange(ROWS, dtype=jnp.int32)
    angles = positions.astype(F32)[:, None] * freqs[None, :]
    cosine, sine = jnp.cos(angles), jnp.sin(angles)
    none = jnp.zeros((ROWS, half), F32)
    rest = jnp.zeros((ROWS, HD - 2 * half), F32)
    tiles = [
        jnp.concatenate([cosine, cosine, rest + 1.0], axis=1),
        jnp.concatenate([none, sine, rest], axis=1),
        jnp.concatenate([-sine, none, rest], axis=1),
    ]
    tab = jnp.stack([jnp.concatenate([tile, tile], axis=1) for tile in tiles])
    return tab, jnp.stack([cosine.T, sine.T])


def body(
    inputs, cotangent, ln_gain, ln_bias, qkv_weight, qkv_bias, out_weight, out_bias,
    fc_in_weight, fc_in_bias, fc_out_weight,
):
    pipe = lax.axis_index("pipe")
    ctx = lax.axis_index("ctx")
    tab, tabt = rope_tables(ctx // 2)
    mine, theirs, smalls = share_weights(
        qkv_weight[0], out_weight[0], fc_in_weight[0], fc_out_weight[0], ln_gain[0], ln_bias[0],
        qkv_bias[0], fc_in_bias, out_bias,
    )
    slabs = mine, theirs.reshape(SLAB, D)

    x = lax.dynamic_index_in_dim(inputs, pipe, 0, keepdims=False)
    g = lax.dynamic_index_in_dim(cotangent, pipe, 0, keepdims=False)
    middle, *kept0 = forward(0, x, slabs, smalls, tab)
    upper, *kept1 = forward(1, middle, slabs, smalls, tab)
    g, wg1, sg1 = backward(1, g, kept1, slabs, smalls, tab, tabt)
    g, wg0, sg0 = backward(0, g, kept0, slabs, smalls, tab, tabt)

    lower_pipe = pipe == 0
    sent = jnp.where(lower_pipe, upper, g)
    held = jnp.where(lower_pipe, g, upper)
    got = lax.ppermute(sent, "pipe", [(0, 1), (1, 0)])
    boundary = jnp.stack([jnp.where(lower_pipe, held, got), jnp.where(lower_pipe, got, held)])[None]

    whole, sums = share_grads(
        wg0.reshape(CHIPS, PIECE, D), wg1.reshape(CHIPS, PIECE, D), sg0, sg1
    )
    g_qkv, g_out, g_in, g_down, g_gain, g_shift, g_qkv_b, g_out_b, g_in_b = finish(
        whole.reshape(2, SLAB, D), sums
    )
    return (
        boundary,
        g_gain[None],
        g_shift[None],
        g_qkv[None],
        g_qkv_b[None],
        g_out[None],
        g_out_b,
        g_in[None],
        g_in_b,
        g_down[None],
    )


def solution(mesh):
    return jax.shard_map(
        body,
        mesh=mesh,
        in_specs=(
            P(None, "ctx", "tensor"),
            P(None, "ctx", "tensor"),
            P("pipe", None, None),
            P("pipe", None, None),
            P("pipe", None, None, "tensor"),
            P("pipe", None, "tensor"),
            P("pipe", "tensor", None),
            P("pipe", "tensor"),
            P("pipe", None, "tensor"),
            P("pipe", "tensor"),
            P("pipe", "tensor", None),
        ),
        out_specs=(
            P("pipe", None, "ctx", "tensor"),
            P("pipe", None, "tensor"),
            P("pipe", None, "tensor"),
            P("pipe", None, None, "tensor"),
            P("pipe", None, "tensor"),
            P("pipe", "tensor", None),
            P("pipe", "tensor"),
            P("pipe", None, "tensor"),
            P("pipe", "tensor"),
            P("pipe", "tensor", None),
        ),
        check_vma=False,
    )
```

time: 1380 us -> 333 us (0.24)
  waiting for transfers between devices: 704 us -> 0.01 us
  Pallas kernels: 0 us -> 325 us
  matrix products: 240 us -> 0 us
  blocking collectives: 160 us -> 0 us
  local copies, waits for them, and re-layouts: 155 us -> 2.79 us
  other arithmetic: 86.3 us -> 2.81 us
  between operations: 16.7 us -> 0.86 us
    pallas_call x0 -> x7, Pallas kernels: none -> 325 us  [the longest x2 102 us: backward(): pl.pallas_call(functools.partial(backward_kernel, l), name=f'layer_{l}_ba...]
    dot_general x57 -> x0, matrix products: 240 us -> none  [the longest x6 37.5 us: masked_scores(): jnp.einsum('chd,shd->hcs', query_heads, key_heads, preferred_element_type...]
    all_gather x6 -> x0, waiting for transfers between devices: 236 us -> none  [the longest x3 129 us: layer_forward(): lax.all_gather(keys, 'ctx', axis=0, tiled=True)]
    reduce_scatter x3 -> x0, waiting for transfers between devices: 230 us -> none  [layer_backward(): lax.psum_scatter(value_full.astype(jnp.bfloat16), 'ctx', scatter_dimensio...]
    unnamed x34 -> x0, waiting for transfers between devices: 225 us -> none
    psum x1 -> x0, blocking collectives: 124 us -> none  [body(): lax.psum(as_sent(totals), 'ctx')]
    unnamed x365 -> x9, local copies, waits for them, and re-layouts: 66.4 us -> 1.31 us
    all_gather x6 -> x0, blocking collectives: 35.3 us -> none  [the longest x3 18.2 us: layer_forward(): whole = lax.all_gather(entry, 'tensor', axis=1, tiled=True)]
  transfers between devices with their start and end apart: 26 -> 1, of which waited for: 23 -> 0; matrix products, arithmetic and copies ran while one was open for 17% -> 0% of each run, Pallas kernels for 0% -> 27%
where the time goes in v1:
time: 333 us
  Pallas kernels  325 us (98%)
    pallas_call x2, Pallas kernels, backward(): pl.pallas_call(functools.partial(backward_kernel, l), name=f'layer_{l}_ba...  102 us
    pallas_call x2, Pallas kernels, forward(): pl.pallas_call(functools.partial(forward_kernel, l), name=f'layer_{l}_for...  99.5 us
    pallas_call x1, Pallas kernels, share_grads(): pl.pallas_call(grads_kernel, name='share_grads', out_shape=(shape((2, CHI...  80.8 us
    pallas_call x1, Pallas kernels, share_weights(): pl.pallas_call(weights_kernel, name='share_weights', out_shape=(shape((SL...  34.7 us
    pallas_call x1, Pallas kernels, finish(): pl.pallas_call(finish_kernel, name='finish', out_shape=(shape((3, D, 384)...  8.23 us
  transfers between devices with their start and end apart: 1, of which 0 were waited for; matrix products, arithmetic and copies ran while one was open for 0% of the time, Pallas kernels for 27%

profile of v1, /device:TPU:1, one launch (start us, length us, event | category | flops | bytes accessed | tf_op | source)
XLA Modules:
  0.0 332.6 jit_solution(13440248707398156890)
XLA Ops:
  0.6 0.0 copy-start.3
  0.7 0.0 copy-start.2
  0.7 0.1 multiply_cosine_fusion.1
  0.8 0.5 multiply_cosine_fusion
  1.4 0.2 concatenate.17
  1.7 0.2 concatenate.16
  1.9 0.2 concatenate.15
  2.2 0.0 copy-done.3
  2.2 0.0 copy-done.2
  2.2 0.7 dynamic-slice_bitcast_fusion
  2.9 0.8 pad_maximum_fusion.tab
  3.7 34.7 %share_weights.1 = (bf16[2304,768]{1,0:T(8,128)(2,1)}, bf16[16,144,768]{2,1,0:T(8,128)(2,1)}, bf16[2,16,768]{2,1,0:T(8,128)(2,1)}) custom-call(bf16[3,768,384]{2,1,0:T(8,128)(2,1)} %bitcast.40, bf16[384,768]{1,0:T(8,128)(2,1)} %bitcast.41, bf16[768,1536]{1,0:T(8,128)(2,1)} %bitcast.38, bf16[1536,768]{1,0:T(8,128)(2,1)} %bitcast.39, bf16[2,768]{1,0:T(2,128)(2,1)} %bitcast.46, ...), custom_call_target="tpu_custom_call" | custom-call | tf_op jit(solution)/shard_map/share_weights/pallas_call | solution.py:743
  38.4 49.8 %layer_0_forward.1 = (bf16[128,384]{1,0:T(8,128)(2,1)}, bf16[2,256,384]{2,1,0:T(8,128)(2,1)}, bf16[16,256,384]{2,1,0:T(8,128)(2,1)}, bf16[3,256,128]{2,1,0:T(8,1...) custom-call(bf16[128,384]{1,0:T(8,128)(2,1)} %get-tuple-element.105.x_ref, ...), custom_call_target="tpu_custom_call" | custom-call | tf_op jit(solution)/shard_map/layer_0_forward/pallas_call | solution.py:763
  88.2 49.7 %layer_1_forward.1 = (bf16[128,384]{1,0:T(8,128)(2,1)}, bf16[2,256,384]{2,1,0:T(8,128)(2,1)}, bf16[16,256,384]{2,1,0:T(8,128)(2,1)}, bf16[3,256,128]{2,1,0:T(8,1...) custom-call(bf16[128,384]{1,0:T(8,128)(2,1)} %get-tuple-element.47.x_ref, ...), custom_call_target="tpu_custom_call" | custom-call | tf_op jit(solution)/shard_map/layer_1_forward/pallas_call | solution.py:763
  137.9 0.6 pad_maximum_fusion.1.tabt
  138.5 53.4 %layer_1_backward.1 = (bf16[128,384]{1,0:T(8,128)(2,1)}, bf16[2304,768]{1,0:T(8,128)(2,1)}, f32[8,768]{1,0:T(8,128)}) custom-call(bf16[128,384]{1,0:T(8,128)(2,1)} %get-tuple-element.106.g_ref, bf16[2,256,384]{2,1,0:T(8,128)(2,1)} %get-tuple-element.48.xg, bf16[2304,768]{1,0:T(8,128)(2,1)} %get-tuple-element.44.slab, bf16[2304,768]{1,0:T(8,128)(2,1)} %bitcast.33, ...), custom_call_target="tpu_custom_call" | custom-call | tf_op jit(solution)/shard_map/layer_1_backward/pallas_call | solution.py:804
  191.9 48.7 %layer_0_backward.1 = (bf16[128,384]{1,0:T(8,128)(2,1)}, bf16[2304,768]{1,0:T(8,128)(2,1)}, f32[8,768]{1,0:T(8,128)}) custom-call(bf16[128,384]{1,0:T(8,128)(2,1)} %get-tuple-element.54.g_ref, bf16[2,256,384]{2,1,0:T(8,128)(2,1)} %get-tuple-element.55.xg, bf16[2304,768]{1,0:T(8,128)(2,1)} %get-tuple-element.44.slab, bf16[2304,768]{1,0:T(8,128)(2,1)} %bitcast.34, ...), custom_call_target="tpu_custom_call" | custom-call | tf_op jit(solution)/shard_map/layer_0_backward/pallas_call | solution.py:804
  240.6 0.8 collective-permute-start
  241.5 80.8 %share_grads.1 = (bf16[2,16,144,768]{3,2,1,0:T(8,128)(2,1)}, f32[2,8,768]{2,1,0:T(8,128)}) custom-call(bf16[16,144,768]{2,1,0:T(8,128)(2,1)} %bitcast.37, bf16[16,144,768]{2,1,0:T(8,128)(2,1)} %bitcast.36, f32[8,768]{1,0:T(8,128)} %get-tuple-element.65.sg0, f32[8,768]{1,0:T(8,128)} %get-tuple-element.66.sg1), custom_call_target="tpu_custom_call" | custom-call | tf_op jit(solution)/shard_map/share_grads/pallas_call | solution.py:832
  322.3 0.0 copy-start.1
  322.3 8.2 %finish.1 = (f32[3,768,384]{2,1,0:T(8,128)}, f32[384,768]{1,0:T(8,128)}, f32[768,1536]{1,0:T(8,128)}, f32[1536,768]{1,0:T(8,128)}, f32[2,384]{1,0:T(2,128)}, /*i...) custom-call(bf16[2,2304,768]{2,1,0:T(8,128)(2,1)} %bitcast.35, ...), custom_call_target="tpu_custom_call" | custom-call | tf_op jit(solution)/shard_map/finish/pallas_call | solution.py:922
  330.6 1.3 copy.23
  331.8 0.0 collective-permute-done
  331.9 0.7 maximum_bitcast_fusion
  (10 shorter events, 0.1 us)
Async XLA Ops:
  0.6 1.6 copy-start.3
  0.7 1.6 copy-start.2
  191.9 48.7 %copy-start = (bf16[128,384]{1,0:T(8,128)(2,1)S(1)}, bf16[128,384]{1,0:T(8,128)(2,1)}, u32[]{:S(2)}) copy-start(bf16[128,384]{1,0:T(8,128)(2,1)} %get-tuple-element.62) | copy-start | bytes 294916
  240.6 91.2 %collective-permute-start = (bf16[128,384]{1,0:T(8,128)(2,1)S(1)}, bf16[128,384]{1,0:T(8,128)(2,1)S(1)}, u32[]{:S(2)}, u32[]{:S(2)}) collective-permute-start(bf16[128,384]{1,0:T(8,128)(2,1)S(1)} %broadcast_select_fusion), channel_id=1, source_target_pairs={{0,64},{64,0},{1,65},{65,1},{2,66},{66,2},{3,67},{67,3},{4,68},{68... | collective-permute-start | bytes 294920 | tf_op jit(solution)/shard_map/ppermute | solution.py:990
  322.3 9.5 %copy-start.1 = (bf16[128,384]{1,0:T(8,128)(2,1)S(1)}, bf16[128,384]{1,0:T(8,128)(2,1)}, u32[]{:S(2)}) copy-start(bf16[128,384]{1,0:T(8,128)(2,1)} %get-tuple-element.61) | copy-start | bytes 294916

commit v2 on v1

--- a/solution.py
+++ b/solution.py
@@ -99,10 +99,18 @@
     return (pl.ds(h * 128 + start, size), pl.ds(0, 384))
 
 
-def slab_view(h, part):
-    cut = (80, 64)[h]
-    start, size = {"all": (0, PIECE), 0: (0, cut), 1: (cut, PIECE - cut)}[part]
-    return (pl.ds(start, size), pl.ds(h * 384, 384))
+def slab_view(h, part, base=0, rows=PIECE):
+    cut = (rows // 2 + 8) // 16 * 16
+    cut = rows - cut if h else cut
+    start, size = {"all": (0, rows), 0: (0, cut), 1: (cut, rows - cut)}[part]
+    return (pl.ds(base + start, size), pl.ds(h * 384, 384))
+
+
+PARTS = ((0, 80), (80, 64))
+
+
+def part_view(i):
+    return lambda h, part: slab_view(h, part, *PARTS[i])
 
 
 class Gather:
@@ -126,10 +134,14 @@
         self.links.arrived(key, self.ref(du, dv, h, part), self.dev(along_u, step, h))
 
     def begin(self):
-        for along_u in (True, False):
-            for h in (0, 1):
-                for step in (1, -1):
-                    self.snd(h, along_u, step, 0, 0, "all")
+        for h in (0, 1):
+            for step in (1, -1):
+                self.snd(h, True, step, 0, 0, "all")
+
+    def own_line(self):
+        for h in (0, 1):
+            for step in (1, -1):
+                self.snd(h, False, step, 0, 0, "all")
 
     def first(self):
         for h in (0, 1):
@@ -157,24 +169,31 @@
             for step, part in ((1, 0), (-1, 1)):
                 self.rcv(h, False, step, du, -2 * step, part)
 
-    def run(self, done=lambda a, b: None):
-        self.begin()
-        done(0, 0)
-        self.first()
-        self.second()
-        for stage, du, slots in (
-            (self.third, 0, ORDER_F[0:4]),
-            (self.third, -1, ORDER_F[4:5]),
-            (self.third, 1, ORDER_F[5:8]),
-            (self.third, 2, ()),
-            (self.fourth, 0, ORDER_F[8:10]),
-            (self.fourth, -1, ORDER_F[10:12]),
-            (self.fourth, 1, ORDER_F[12:14]),
-            (self.fourth, 2, ORDER_F[14:15]),
-        ):
-            stage(du)
-            for a, b in slots:
-                done(a, b)
+
+def gather_parts(parts, arrived, done=lambda a, b: None):
+    for i, part in enumerate(parts):
+        arrived(i)
+        part.begin()
+    done(0, 0)
+    for part in parts:
+        part.first()
+        part.own_line()
+    for part in parts:
+        part.second()
+    for stage, du, slots in (
+        ("third", 0, ORDER_F[0:4]),
+        ("third", -1, ORDER_F[4:5]),
+        ("third", 1, ORDER_F[5:8]),
+        ("third", 2, ()),
+        ("fourth", 0, ORDER_F[8:10]),
+        ("fourth", -1, ORDER_F[10:12]),
+        ("fourth", 1, ORDER_F[12:14]),
+        ("fourth", 2, ORDER_F[14:15]),
+    ):
+        for part in parts:
+            getattr(part, stage)(du)
+        for a, b in slots:
+            done(a, b)
 
 
 class Scatter:
@@ -242,6 +261,18 @@
         mine = self.ref(0, 0, h, "all")
         return mine[...].astype(F32) + one[...].astype(F32) + two[...].astype(F32)
 
+    def begin(self):
+        for du in (2, -1, 1, 0):
+            for h in (0, 1):
+                for step in (1, -1):
+                    self.v1(h, step, du)
+
+    def middle(self):
+        for du in (2, -1, 1, 0):
+            for h in (0, 1):
+                for step in (1, -1):
+                    self.v2(h, step, du)
+
     def tail_one(self):
         for h in (0, 1):
             self.vsum(h, 2)
@@ -267,32 +298,40 @@
 
 def mates_gather(place, links, own, full, tag):
     rows = pl.ds(pl.multiple_of(place.core * 128, 128), 128)
-    for r in (1, 2, 3):
+    for r in (2, 1):
         device = place.mate(r)[2]
         links.send((tag, r), lambda device=device: (own, full.at[place.tensor, rows], device))
     full[place.tensor, rows] = own[...]
 
 
 def mates_gathered(place, links, full, tag):
-    for r in (1, 2, 3):
-        t, c, device = place.mate(r)
-        links.arrived((tag, r), full.at[t, pl.ds(pl.multiple_of(c * 128, 128), 128)], device)
+    rows = pl.ds(pl.multiple_of(place.core * 128, 128), 128)
+    others = pl.ds(pl.multiple_of(128 - place.core * 128, 128), 128)
+    far, sibling = place.mate(2)[2], place.mate(1)[2]
+    links.arrived((tag, 2), full.at[1 - place.tensor, rows], far)
+    passed = full.at[1 - place.tensor, rows]
+    links.send((tag, 3), lambda: (passed, passed, sibling))
+    links.arrived((tag, 1), full.at[place.tensor, others], sibling)
+    links.arrived((tag, 3), full.at[1 - place.tensor, others], sibling)
 
 
 def mates_scatter(place, links, part, rounded, landing, tag):
-    rounded[...] = part[...].astype(BF)
-    for r in (1, 2, 3):
-        t, c, device = place.mate(r)
-        src = rounded.at[t, pl.ds(pl.multiple_of(c * 128, 128), 128)]
-        links.send((tag, r), lambda r=r, src=src, device=device: (src, landing.at[r - 1], device))
-
-
-def mates_scattered(place, links, part, landing, tag):
-    total = part[place.tensor, pl.ds(pl.multiple_of(place.core * 128, 128), 128)]
-    for r in (1, 2, 3):
-        links.arrived((tag, r), landing.at[r - 1], place.mate(r)[2])
-        total = total + landing[r - 1].astype(F32)
-    return total
+    others = pl.ds(pl.multiple_of(128 - place.core * 128, 128), 128)
+    rounded[:, others] = part[:, others].astype(BF)
+    device = place.mate(1)[2]
+    links.send((tag, 1), lambda: (rounded.at[:, others], landing.at[pl.ds(0, 2)], device))
+
+
+def mates_scattered(place, links, part, rounded, landing, tag):
+    rows = pl.ds(pl.multiple_of(place.core * 128, 128), 128)
+    links.arrived((tag, 1), landing.at[pl.ds(0, 2)], place.mate(1)[2])
+    away = part[1 - place.tensor, rows] + landing[1 - place.tensor].astype(F32)
+    rounded[1 - place.tensor, rows] = away.astype(BF)
+    device = place.mate(2)[2]
+    links.send((tag, 2), lambda: (rounded.at[1 - place.tensor, rows], landing.at[2], device))
+    total = part[place.tensor, rows] + landing[place.tensor].astype(F32)
+    links.arrived((tag, 2), landing.at[2], device)
+    return total + landing[2].astype(F32)
 
 
 def normalize(values):
@@ -356,14 +395,19 @@
     for load in loads[1:]:
         load.wait()
     device = place.partner()
-    piece = pl.ds(pl.multiple_of(place.chip * PIECE, PIECE), PIECE)
-    links.send("slab", lambda: (own.at[piece], buf.at[place.chip], device))
+    for i, (base, rows) in enumerate(PARTS):
+        src = own.at[pl.ds(pl.multiple_of(place.chip * PIECE + base, 16), rows)]
+        dst = buf.at[place.chip, pl.ds(base, rows)]
+        links.send(("slab", i), lambda src=src, dst=dst: (src, dst, device))
     got_small[0] = rounded
     links.send("small", lambda: (got_small.at[0], got_small.at[1], device))
     keep = pltpu.make_async_copy(own, mine, local.at[6])
     keep.start()
-    links.arrived("slab", buf.at[place.chip], device)
-    Gather(place, links, buf, slab_view).run()
+
+    def piece(i):
+        links.arrived(("slab", i), buf.at[place.chip, pl.ds(*PARTS[i])], device)
+
+    gather_parts([Gather(place, links, buf, part_view(i), i) for i in range(2)], piece)
     store = pltpu.make_async_copy(buf, theirs, local.at[7])
     store.start()
     links.arrived("small", got_small.at[1], device)
@@ -390,7 +434,7 @@
     place = Place()
     links = Links(send_sems, recv_sems)
     load = load_layer(l, place, slab, slab2, w, local.at[0])
-    place.greet(mates=(1, 2, 3))
+    place.greet(mates=(1, 2))
     mates_gather(place, links, x_ref, xg, "x")
     vectors = small[l].astype(F32)
     mates_gathered(place, links, xg, "x")
@@ -417,6 +461,7 @@
     q_o[1] = jnp.where(high, qa, zero)
     q_o[2] = jnp.where(low, qb, zero)
     gather.first()
+    gather.own_line()
     inner = dot(second, w[I0:U0, :]) + vectors[5:6]
     inner_o[...] = inner
     act = (inner * (0.5 * (1.0 + lax.erf(inner * (2.0**-0.5))))).astype(BF)
@@ -483,24 +528,36 @@
     part[0] = part[0] + branch[:, 0:384]
     part[1] = part[1] + branch[:, 384:768]
     mates_scatter(place, links, part, rounded, landing, "y")
-    y = mates_scattered(place, links, part, landing, "y")
+    y = mates_scattered(place, links, part, rounded, landing, "y")
     y_ref[...] = (y + x_ref[...].astype(F32) + vectors[6:7, 0:384]).astype(BF)
     store.wait()
     links.finish()
 
 
 def backward_kernel(
-    l, g_ref, xg, slab, slab2, small, tab, tabt, kv, q, ot, lse, inner, gx_ref, wg, sg,
-    w, gg, kvb, dkv, dqt, do, first, second, act, slope, part, rounded, landing,
-    r1, r2, u1, u2, send_sems, recv_sems, local,
+    l, g_ref, xg, slab, slab2, small, tab, tabt, kv, q, ot, lse, inner, *refs
 ):
+    if l == 0:
+        above, gx_ref, wg, sg, piece, *refs = refs
+        *refs, above_v, a1, a2, b1, b2 = refs
+    else:
+        gx_ref, wg, sg, *refs = refs
+    (w, gg, kvb, dkv, dqt, do, first, second, act, slope, part, rounded, landing,
+     r1, r2, u1, u2, send_sems, recv_sems, local) = refs
     place = Place()
     links = Links(send_sems, recv_sems)
     load = load_layer(l, place, slab, slab2, w, local.at[0])
     load_kv = pltpu.make_async_copy(kv, kvb, local.at[1])
     load_kv.start()
-    place.greet(mates=(1, 2, 3))
+    if l == 0:
+        load_above = pltpu.make_async_copy(above, above_v, local.at[2])
+        load_above.start()
+    place.greet(mates=(1, 2))
     mates_gather(place, links, g_ref, gg, "g")
+    if l == 0:
+        load_above.wait()
+        upper = Scatter(place, links, above_v, slab_view, a1, a2, b1, b2, "w")
+        upper.begin()
     vectors = small[l].astype(F32)
     x = jnp.concatenate([xg[0], xg[1]], axis=1).astype(F32)
     normed, scale = normalize(x)
@@ -524,6 +581,8 @@
     delta = [
         jnp.sum(dot_t[s : s + 64], axis=0, keepdims=True) for s in (64, 0, 128)
     ]
+    if l == 0:
+        upper.middle()
     load_kv.wait()
     dqt[...] = jnp.zeros_like(dqt)
     scatter = Scatter(place, links, dkv, kv_view, r1, r2, u1, u2)
@@ -581,12 +640,18 @@
     g = jnp.concatenate([gg[0], gg[1]], axis=1)
     grad_inner = (dot(g, w[U0:SLAB, :], NT) * slope[...]).astype(BF)
     wg[U0:SLAB, :] = dot(act[...], g, TN).astype(BF)
+    if l == 0:
+        upper.tail_one()
     scatter.tail_one()
     wg[I0:U0, :] = dot(second[...], grad_inner, TN).astype(BF)
+    if l == 0:
+        upper.tail_two()
     scatter.tail_two()
     grad_second = dot(grad_inner, w[I0:U0, :], NT)
     wg[O0:I0, :] = dot(ot[...].astype(BF), g).astype(BF)
     scatter.tail_three()
+    if l == 0:
+        upper.tail_three()
     sg[0:1, :] = jnp.sum(grad_second * normed, axis=0, keepdims=True)
     sg[1:2, :] = jnp.sum(grad_second, axis=0, keepdims=True)
     sg[2:3, :] = jnp.sum(grad_inner.astype(F32), axis=0, keepdims=True)
@@ -623,19 +688,22 @@
     part[0] = grad_x[:, 0:384]
     part[1] = grad_x[:, 384:768]
     mates_scatter(place, links, part, rounded, landing, "gx")
-    grad = mates_scattered(place, links, part, landing, "gx")
+    if l == 0:
+        for h in (0, 1):
+            piece[:, h * 384 : h * 384 + 384] = upper.last(h)
+    grad = mates_scattered(place, links, part, rounded, landing, "gx")
     gx_ref[...] = (grad + g_ref[...].astype(F32)).astype(BF)
     links.finish()
 
 
 def grads_kernel(
-    wg0, wg1, sg0, sg1, out, out_small, buf, own, other, piece, got, r1, r2, u1, u2,
+    wg0, piece1, sg0, sg1, out, out_small, buf, own, piece, got, r1, r2, u1, u2,
     sm, along_x, along_z, across, beside, send_sems, recv_sems, local
 ):
     place = Place()
     links = Links(send_sems, recv_sems)
-    load_theirs = load_layer(1, place, wg0, wg1, other, local.at[0])
-    load_mine = load_layer(0, place, wg0, wg1, own, local.at[1])
+    load = pltpu.make_async_copy(wg0, own, local.at[0])
+    load.start()
     place.greet(mates=(1, 2, 3), partner=True, far=True)
     sm[0, 0] = sg0[...]
     sm[0, 1] = sg1[...]
@@ -675,42 +743,40 @@
         out_small[place.core] = jnp.where(norm, total, sm[3, 0])
         out_small[1 - place.core] = jnp.where(norm, total, beside[0])
 
-    sums = []
-    for i, ref in ((0, other), (1, own)):
-        (load_theirs, load_mine)[i].wait()
-        scatter = Scatter(place, links, ref, slab_view, r1.at[i], r2.at[i], u1.at[i], u2.at[i], i)
-        sums.append(scatter)
-        for du in (2, -1, 1, 0):
-            for h in (0, 1):
-                for s in (1, -1):
-                    scatter.v1(h, s, du)
+    load.wait()
+    scatter = Scatter(place, links, own, slab_view, r1, r2, u1, u2)
+    scatter.begin()
     small_z()
-    for scatter in sums:
-        for du in (2, -1, 1, 0):
-            for h in (0, 1):
-                for s in (1, -1):
-                    scatter.v2(h, s, du)
+    scatter.middle()
     small_pipe()
+    scatter.tail_one()
+    scatter.tail_two()
+    scatter.tail_three()
+    small_mates()
     device = place.partner()
-    for i, scatter in enumerate(sums):
-        scatter.tail_one()
-        scatter.tail_two()
-        scatter.tail_three()
-        for h in (0, 1):
-            piece[i, :, h * 384 : h * 384 + 384] = scatter.last(h)
-        if i == 0:
-            got[0] = piece[0].astype(BF)
-            links.send("piece", lambda: (got.at[0], got.at[1], device))
-    links.arrived("piece", got.at[1], device)
-    small_mates()
-    buf[place.core, place.chip] = (piece[1] + got[1].astype(F32)).astype(BF)
+    lower_pipe = place.pipe == 0
+    for h in (0, 1):
+        lanes = pl.ds(h * 384, 384)
+        zero, one = scatter.last(h), piece1[:, lanes]
+        piece[:, lanes] = jnp.where(lower_pipe, zero, one)
+        got[0, :, lanes] = jnp.where(lower_pipe, one, zero).astype(BF)
+    for i, (base, rows) in enumerate(PARTS):
+        span = pl.ds(base, rows)
+        links.send(("piece", i), lambda span=span: (got.at[0, span], got.at[1, span], device))
+
+    def whole(i):
+        span = pl.ds(*PARTS[i])
+        links.arrived(("piece", i), got.at[1, span], device)
+        buf[place.core, place.chip, span] = (piece[span] + got[1, span].astype(F32)).astype(BF)
+
     sibling = place.mate(1)[2]
 
     def pass_on(a, b):
         ref = lambda: buf.at[place.core, place.slot(a, b)]
         links.send(("core", a, b), lambda: (ref(), ref(), sibling))
 
-    Gather(place, links, buf.at[place.core], slab_view, "g").run(pass_on)
+    parts = [Gather(place, links, buf.at[place.core], part_view(i), i) for i in range(2)]
+    gather_parts(parts, whole, pass_on)
     keep = pltpu.make_async_copy(buf.at[place.core], out.at[place.core], local.at[0])
     keep.start()
     small_last()
@@ -753,7 +819,7 @@
             pltpu.VMEM((384, D), BF),
             pltpu.VMEM((16, D), F32),
             pltpu.VMEM((2, 16, D), BF),
-            *sems(48, 8),
+            *sems(96, 8),
         ],
         compiler_params=params(0),
     )(*args)
@@ -790,23 +856,29 @@
     )(x, *slab, small, tab)
 
 
-def landing_shapes(rows, part, lead=()):
+def landing_shapes(rows, part):
     return [
-        pltpu.VMEM((*lead, 2, 2, 4, part, 384), BF),
-        pltpu.VMEM((*lead, 2, 2, 4, rows, 384), BF),
-        pltpu.VMEM((*lead, 2, 2, part, 384), BF),
-        pltpu.VMEM((*lead, 2, 2, rows, 384), BF),
+        pltpu.VMEM((2, 2, 4, part, 384), BF),
+        pltpu.VMEM((2, 2, 4, rows, 384), BF),
+        pltpu.VMEM((2, 2, part, 384), BF),
+        pltpu.VMEM((2, 2, rows, 384), BF),
     ]
 
 
-def backward(l, g, kept, slab, small, tab, tabt):
+def backward(l, g, kept, slab, small, tab, tabt, above=()):
     xg, kv, q, ot, lse, inner = kept
+    extra = [VMEM] if l == 0 else []
     return pl.pallas_call(
         functools.partial(backward_kernel, l),
         name=f"layer_{l}_backward",
-        out_shape=(shape((128, 384)), shape((SLAB, D)), shape((8, D), F32)),
-        in_specs=[VMEM, VMEM, ANY, ANY, VMEM, VMEM, VMEM, ANY, VMEM, VMEM, VMEM, VMEM],
-        out_specs=(VMEM, VMEM, VMEM),
+        out_shape=(
+            shape((128, 384)),
+            shape((SLAB, D)),
+            shape((8, D), F32),
+            *([shape((PIECE, D), F32)] if l == 0 else []),
+        ),
+        in_specs=[VMEM, VMEM, ANY, ANY, VMEM, VMEM, VMEM, ANY, VMEM, VMEM, VMEM, VMEM, *([ANY] if l == 0 else [])],
+        out_specs=(VMEM, VMEM, VMEM, *extra),
         scratch_shapes=[
             pltpu.VMEM((SLAB, D), BF),
             pltpu.VMEM((2, ROWS, 384), BF),
@@ -822,10 +894,11 @@
             pltpu.VMEM((2, ROWS, 384), BF),
             pltpu.VMEM((3, 128, 384), BF),
             *landing_shapes(128, 64),
-            *sems(56, 2),
+            *sems(96, 3),
+            *([pltpu.VMEM((CHIPS, PIECE, D), BF), *landing_shapes(PIECE, 80)] if l == 0 else []),
         ],
         compiler_params=params(3 + l),
-    )(g, xg, *slab, small, tab, tabt, kv, q, ot, lse, inner)
+    )(g, xg, *slab, small, tab, tabt, kv, q, ot, lse, inner, *above)
 
 
 def share_grads(*args):
@@ -833,21 +906,20 @@
         grads_kernel,
         name="share_grads",
         out_shape=(shape((2, CHIPS, PIECE, D)), shape((2, 8, D), F32)),
-        in_specs=[ANY, ANY, VMEM, VMEM],
+        in_specs=[ANY, VMEM, VMEM, VMEM],
         out_specs=(ANY, VMEM),
         scratch_shapes=[
             pltpu.VMEM((2, CHIPS, PIECE, D), BF),
             pltpu.VMEM((CHIPS, PIECE, D), BF),
-            pltpu.VMEM((CHIPS, PIECE, D), BF),
-            pltpu.VMEM((2, PIECE, D), F32),
+            pltpu.VMEM((PIECE, D), F32),
             pltpu.VMEM((2, PIECE, D), BF),
-            *landing_shapes(PIECE, 80, (2,)),
+            *landing_shapes(PIECE, 80),
             pltpu.VMEM((4, 2, 8, D), F32),
             pltpu.VMEM((3, 2, 8, D), F32),
             pltpu.VMEM((3, 2, 8, D), F32),
             pltpu.VMEM((8, D), F32),
             pltpu.VMEM((3, 8, D), F32),
-            *sems(160, 2),
+            *sems(176, 2),
         ],
         compiler_params=params(5),
     )(*args)
@@ -982,7 +1054,8 @@
     middle, *kept0 = forward(0, x, slabs, smalls, tab)
     upper, *kept1 = forward(1, middle, slabs, smalls, tab)
     g, wg1, sg1 = backward(1, g, kept1, slabs, smalls, tab, tabt)
-    g, wg0, sg0 = backward(0, g, kept0, slabs, smalls, tab, tabt)
+    above = wg1.reshape(CHIPS, PIECE, D)
+    g, wg0, sg0, piece1 = backward(0, g, kept0, slabs, smalls, tab, tabt, (above,))
 
     lower_pipe = pipe == 0
     sent = jnp.where(lower_pipe, upper, g)
@@ -991,7 +1064,7 @@
     boundary = jnp.stack([jnp.where(lower_pipe, held, got), jnp.where(lower_pipe, got, held)])[None]
 
     whole, sums = share_grads(
-        wg0.reshape(CHIPS, PIECE, D), wg1.reshape(CHIPS, PIECE, D), sg0, sg1
+        wg0.reshape(CHIPS, PIECE, D), piece1, sg0, sg1
     )
     g_qkv, g_out, g_in, g_down, g_gain, g_shift, g_qkv_b, g_out_b, g_in_b = finish(
         whole.reshape(2, SLAB, D), sums

time: 333 us -> 317 us (0.952)
  Pallas kernels: 325 us -> 310 us
    pallas_call x1, Pallas kernels: 80.8 us -> 59.9 us  [share_grads(): pl.pallas_call(grads_kernel, name='share_grads', out_shape=(shape((2, CHI...]
    pallas_call x2, Pallas kernels: 102 us -> 109 us  [backward(): pl.pallas_call(functools.partial(backward_kernel, l), name=f'layer_{l}_ba...]
  transfers between devices with their start and end apart: 1 -> 1, of which waited for: 0 -> 0; matrix products, arithmetic and copies ran while one was open for 0% -> 0% of each run, Pallas kernels for 27% -> 22%
where the time goes in v2:
time: 317 us
  Pallas kernels  310 us (98%)
    pallas_call x2, Pallas kernels, backward(): pl.pallas_call(functools.partial(backward_kernel, l), name=f'layer_{l}_ba...  109 us
    pallas_call x2, Pallas kernels, forward(): pl.pallas_call(functools.partial(forward_kernel, l), name=f'layer_{l}_for...  97.2 us
    pallas_call x1, Pallas kernels, share_grads(): pl.pallas_call(grads_kernel, name='share_grads', out_shape=(shape((2, CHI...  59.9 us
    pallas_call x1, Pallas kernels, share_weights(): pl.pallas_call(weights_kernel, name='share_weights', out_shape=(shape((SL...  35.3 us
    pallas_call x1, Pallas kernels, finish(): pl.pallas_call(finish_kernel, name='finish', out_shape=(shape((3, D, 384)...  8.23 us
  transfers between devices with their start and end apart: 1, of which 0 were waited for; matrix products, arithmetic and copies ran while one was open for 0% of the time, Pallas kernels for 22%

profile of v2, /device:TPU:1, one launch (start us, length us, event | category | flops | bytes accessed | tf_op | source)
XLA Modules:
  0.0 316.9 jit_solution(12663669037135939174)
XLA Ops:
  0.6 0.0 copy-start.3
  0.7 0.0 copy-start.2
  0.7 0.1 multiply_cosine_fusion.1
  0.8 0.5 multiply_cosine_fusion
  1.4 0.2 concatenate.17
  1.7 0.2 concatenate.16
  1.9 0.2 concatenate.15
  2.2 0.0 copy-done.3
  2.2 0.0 copy-done.2
  2.2 0.7 dynamic-slice_bitcast_fusion
  2.9 0.8 pad_maximum_fusion.tab
  3.7 35.3 %share_weights.1 = (bf16[2304,768]{1,0:T(8,128)(2,1)}, bf16[16,144,768]{2,1,0:T(8,128)(2,1)}, bf16[2,16,768]{2,1,0:T(8,128)(2,1)}) custom-call(bf16[3,768,384]{2,1,0:T(8,128)(2,1)} %bitcast.40, bf16[384,768]{1,0:T(8,128)(2,1)} %bitcast.41, bf16[768,1536]{1,0:T(8,128)(2,1)} %bitcast.38, bf16[1536,768]{1,0:T(8,128)(2,1)} %bitcast.39, bf16[2,768]{1,0:T(2,128)(2,1)} %bitcast.46, ...), custom_call_target="tpu_custom_call" | custom-call | tf_op jit(solution)/shard_map/share_weights/pallas_call | solution.py:809
  39.0 46.4 %layer_0_forward.1 = (bf16[128,384]{1,0:T(8,128)(2,1)}, bf16[2,256,384]{2,1,0:T(8,128)(2,1)}, bf16[16,256,384]{2,1,0:T(8,128)(2,1)}, bf16[3,256,128]{2,1,0:T(8,1...) custom-call(bf16[128,384]{1,0:T(8,128)(2,1)} %get-tuple-element.107.x_ref, ...), custom_call_target="tpu_custom_call" | custom-call | tf_op jit(solution)/shard_map/layer_0_forward/pallas_call | solution.py:829
  85.4 50.8 %layer_1_forward.1 = (bf16[128,384]{1,0:T(8,128)(2,1)}, bf16[2,256,384]{2,1,0:T(8,128)(2,1)}, bf16[16,256,384]{2,1,0:T(8,128)(2,1)}, bf16[3,256,128]{2,1,0:T(8,1...) custom-call(bf16[128,384]{1,0:T(8,128)(2,1)} %get-tuple-element.48.x_ref, ...), custom_call_target="tpu_custom_call" | custom-call | tf_op jit(solution)/shard_map/layer_1_forward/pallas_call | solution.py:829
  136.2 0.6 pad_maximum_fusion.1.tabt
  136.8 53.3 %layer_1_backward.1 = (bf16[128,384]{1,0:T(8,128)(2,1)}, bf16[2304,768]{1,0:T(8,128)(2,1)}, f32[8,768]{1,0:T(8,128)}) custom-call(bf16[128,384]{1,0:T(8,128)(2,1)} %get-tuple-element.108.g_ref, bf16[2,256,384]{2,1,0:T(8,128)(2,1)} %get-tuple-element.49.xg, bf16[2304,768]{1,0:T(8,128)(2,1)} %get-tuple-element.45.slab, bf16[2304,768]{1,0:T(8,128)(2,1)} %bitcast.33, ...), custom_call_target="tpu_custom_call" | custom-call | tf_op jit(solution)/shard_map/layer_1_backward/pallas_call | solution.py:871
  190.1 0.0 copy-start
  190.1 55.6 %layer_0_backward.1 = (bf16[128,384]{1,0:T(8,128)(2,1)}, bf16[2304,768]{1,0:T(8,128)(2,1)}, f32[8,768]{1,0:T(8,128)}, f32[144,768]{1,0:T(8,128)}) custom-call(bf16[128,384]{1,0:T(8,128)(2,1)} %get-tuple-element.55.g_ref, bf16[2,256,384]{2,1,0:T(8,128)(2,1)} %get-tuple-element.56.xg, bf16[2304,768]{1,0:T(8,128)(2,1)} %get-tuple-element.45.slab, ...), custom_call_target="tpu_custom_call" | custom-call | tf_op jit(solution)/shard_map/layer_0_backward/pallas_call | solution.py:871
  245.8 0.9 collective-permute-start
  246.7 59.9 %share_grads.1 = (bf16[2,16,144,768]{3,2,1,0:T(8,128)(2,1)}, f32[2,8,768]{2,1,0:T(8,128)}) custom-call(bf16[16,144,768]{2,1,0:T(8,128)(2,1)} %bitcast.37, f32[144,768]{1,0:T(8,128)} %get-tuple-element.66.piece1, f32[8,768]{1,0:T(8,128)} %get-tuple-element.67.sg0, f32[8,768]{1,0:T(8,128)} %get-tuple-element.68.sg1), custom_call_target="tpu_custom_call" | custom-call | tf_op jit(solution)/shard_map/share_grads/pallas_call | solution.py:905
  306.7 8.2 %finish.1 = (f32[3,768,384]{2,1,0:T(8,128)}, f32[384,768]{1,0:T(8,128)}, f32[768,1536]{1,0:T(8,128)}, f32[1536,768]{1,0:T(8,128)}, f32[2,384]{1,0:T(2,128)}, /*i...) custom-call(bf16[2,2304,768]{2,1,0:T(8,128)(2,1)} %bitcast.35, ...), custom_call_target="tpu_custom_call" | custom-call | tf_op jit(solution)/shard_map/finish/pallas_call | solution.py:994
  314.9 1.3 copy.23
  316.2 0.0 collective-permute-done
  316.2 0.7 maximum_bitcast_fusion
  (10 shorter events, 0.1 us)
Async XLA Ops:
  0.6 1.6 copy-start.3
  0.7 1.6 copy-start.2
  190.1 55.7 %copy-start = (bf16[128,384]{1,0:T(8,128)(2,1)S(1)}, bf16[128,384]{1,0:T(8,128)(2,1)}, u32[]{:S(2)}) copy-start(bf16[128,384]{1,0:T(8,128)(2,1)} %get-tuple-element.64) | copy-start | bytes 294916
  245.8 70.4 %collective-permute-start = (bf16[128,384]{1,0:T(8,128)(2,1)S(1)}, bf16[128,384]{1,0:T(8,128)(2,1)S(1)}, u32[]{:S(2)}, u32[]{:S(2)}) collective-permute-start(bf16[128,384]{1,0:T(8,128)(2,1)S(1)} %broadcast_select_fusion), channel_id=1, source_target_pairs={{0,64},{64,0},{1,65},{65,1},{2,66},{66,2},{3,67},{67,3},{4,68},{68... | collective-permute-start | bytes 294920 | tf_op jit(solution)/shard_map/ppermute | solution.py:1063
  306.7 9.5 %copy-start.1 = (bf16[128,384]{1,0:T(8,128)(2,1)S(1)}, bf16[128,384]{1,0:T(8,128)(2,1)}, u32[]{:S(2)}) copy-start(bf16[128,384]{1,0:T(8,128)(2,1)} %get-tuple-element.63) | copy-start | bytes 294916

commit v3 on v2

--- a/solution.py
+++ b/solution.py
@@ -427,18 +427,13 @@
 ORDER_B = ((2, 2), (0, 2), (2, 0), (-1, 2), (1, 2), (2, -1), (2, 1), (-1, -1), (-1, 1), (1, -1), (1, 1), (0, -1), (0, 1), (-1, 0), (1, 0))
 
 
-def forward_kernel(
-    l, x_ref, slab, slab2, small, tab, y_ref, xg_o, kv_o, q_o, ot_o, lse_o, inner_o,
-    w, xg, kvb, acc, top, total, part, rounded, landing, send_sems, recv_sems, local,
+def forward_part(
+    l, place, links, load, x_ref, small, tab, y_ref, xg, kvb, q_o, ot_o, lse_o, inner_o,
+    w, acc, top, total, part, rounded, landing,
 ):
-    place = Place()
-    links = Links(send_sems, recv_sems)
-    load = load_layer(l, place, slab, slab2, w, local.at[0])
-    place.greet(mates=(1, 2))
-    mates_gather(place, links, x_ref, xg, "x")
+    mates_gather(place, links, x_ref, xg, ("x", l))
     vectors = small[l].astype(F32)
-    mates_gathered(place, links, xg, "x")
-    xg_o[...] = xg[...]
+    mates_gathered(place, links, xg, ("x", l))
     x = jnp.concatenate([xg[0], xg[1]], axis=1).astype(F32)
     normed, _ = normalize(x)
     first = (normed * vectors[0:1] + vectors[2:3]).astype(BF)
@@ -448,7 +443,7 @@
     for h in range(3):
         tile = kv[:, h * 128 : h * 128 + 128]
         kvb[place.chip, :, h * 128 : h * 128 + 128] = turn(tile, tab, h != 1, h == 1).astype(BF)
-    gather = Gather(place, links, kvb, kv_view)
+    gather = Gather(place, links, kvb, kv_view, ("kv", l))
     gather.begin()
     low, high = lane_mask(True), lane_mask(False)
     qa = dot(first, w[Q0 : Q0 + 128, :], NT) + vectors[4:5, 384:512]
@@ -489,10 +484,10 @@
     def step(n, carry):
         for j, action in (
             (0, lambda: gather.third(0)),
-            (4, lambda: gather.third(-1)),
-            (5, lambda: gather.third(1)),
+            (2, lambda: gather.third(-1)),
+            (4, lambda: gather.third(1)),
+            (6, lambda: gather.third(2)),
             (8, lambda: gather.fourth(0)),
-            (9, lambda: gather.third(2)),
             (10, lambda: gather.fourth(-1)),
             (12, lambda: gather.fourth(1)),
             (14, lambda: gather.fourth(2)),
@@ -515,8 +510,6 @@
         return carry
 
     lax.fori_loop(0, 15, step, 0)
-    store = pltpu.make_async_copy(kvb, kv_o, local.at[1])
-    store.start()
     heads = []
     for h in range(3):
         rows = slice(0, 64) if h == 1 else slice(64, 128)
@@ -527,36 +520,18 @@
     branch = dot(attn.astype(BF), w[O0:I0, :], TN)
     part[0] = part[0] + branch[:, 0:384]
     part[1] = part[1] + branch[:, 384:768]
-    mates_scatter(place, links, part, rounded, landing, "y")
-    y = mates_scattered(place, links, part, rounded, landing, "y")
+    mates_scatter(place, links, part, rounded, landing, ("y", l))
+    y = mates_scattered(place, links, part, rounded, landing, ("y", l))
     y_ref[...] = (y + x_ref[...].astype(F32) + vectors[6:7, 0:384]).astype(BF)
-    store.wait()
-    links.finish()
-
-
-def backward_kernel(
-    l, g_ref, xg, slab, slab2, small, tab, tabt, kv, q, ot, lse, inner, *refs
+
+
+def backward_part(
+    l, place, links, g_ref, xg, small, tab, tabt, kvb, q, ot, lse, inner, gx_ref, wg, sg,
+    w, gg, dkv, dqt, do, first, second, act, slope, part, rounded, landing, r1, r2, u1, u2,
+    upper=None, piece=None,
 ):
-    if l == 0:
-        above, gx_ref, wg, sg, piece, *refs = refs
-        *refs, above_v, a1, a2, b1, b2 = refs
-    else:
-        gx_ref, wg, sg, *refs = refs
-    (w, gg, kvb, dkv, dqt, do, first, second, act, slope, part, rounded, landing,
-     r1, r2, u1, u2, send_sems, recv_sems, local) = refs
-    place = Place()
-    links = Links(send_sems, recv_sems)
-    load = load_layer(l, place, slab, slab2, w, local.at[0])
-    load_kv = pltpu.make_async_copy(kv, kvb, local.at[1])
-    load_kv.start()
-    if l == 0:
-        load_above = pltpu.make_async_copy(above, above_v, local.at[2])
-        load_above.start()
-    place.greet(mates=(1, 2))
-    mates_gather(place, links, g_ref, gg, "g")
-    if l == 0:
-        load_above.wait()
-        upper = Scatter(place, links, above_v, slab_view, a1, a2, b1, b2, "w")
+    mates_gather(place, links, g_ref, gg, ("g", l))
+    if upper is not None:
         upper.begin()
     vectors = small[l].astype(F32)
     x = jnp.concatenate([xg[0], xg[1]], axis=1).astype(F32)
@@ -567,8 +542,7 @@
     cdf = 0.5 * (1.0 + lax.erf(value * (2.0**-0.5)))
     act[...] = (value * cdf).astype(BF)
     slope[...] = cdf + value * jnp.exp(-0.5 * value * value) * 0.3989422804014327
-    load.wait()
-    mates_gathered(place, links, gg, "g")
+    mates_gathered(place, links, gg, ("g", l))
     g = jnp.concatenate([gg[0], gg[1]], axis=1)
     low, high = lane_mask(True), lane_mask(False)
     zero = jnp.zeros((ROWS, 128), BF)
@@ -581,11 +555,10 @@
     delta = [
         jnp.sum(dot_t[s : s + 64], axis=0, keepdims=True) for s in (64, 0, 128)
     ]
-    if l == 0:
+    if upper is not None:
         upper.middle()
-    load_kv.wait()
     dqt[...] = jnp.zeros_like(dqt)
-    scatter = Scatter(place, links, dkv, kv_view, r1, r2, u1, u2)
+    scatter = Scatter(place, links, dkv, kv_view, r1, r2, u1, u2, ("d", l))
 
     def chunk(kk, mask):
         for h in range(3):
@@ -640,17 +613,17 @@
     g = jnp.concatenate([gg[0], gg[1]], axis=1)
     grad_inner = (dot(g, w[U0:SLAB, :], NT) * slope[...]).astype(BF)
     wg[U0:SLAB, :] = dot(act[...], g, TN).astype(BF)
-    if l == 0:
+    if upper is not None:
         upper.tail_one()
     scatter.tail_one()
     wg[I0:U0, :] = dot(second[...], grad_inner, TN).astype(BF)
-    if l == 0:
+    if upper is not None:
         upper.tail_two()
     scatter.tail_two()
     grad_second = dot(grad_inner, w[I0:U0, :], NT)
     wg[O0:I0, :] = dot(ot[...].astype(BF), g).astype(BF)
     scatter.tail_three()
-    if l == 0:
+    if upper is not None:
         upper.tail_three()
     sg[0:1, :] = jnp.sum(grad_second * normed, axis=0, keepdims=True)
     sg[1:2, :] = jnp.sum(grad_second, axis=0, keepdims=True)
@@ -687,12 +660,48 @@
     )
     part[0] = grad_x[:, 0:384]
     part[1] = grad_x[:, 384:768]
-    mates_scatter(place, links, part, rounded, landing, "gx")
-    if l == 0:
+    mates_scatter(place, links, part, rounded, landing, ("gx", l))
+    if upper is not None:
         for h in (0, 1):
             piece[:, h * 384 : h * 384 + 384] = upper.last(h)
-    grad = mates_scattered(place, links, part, rounded, landing, "gx")
+    grad = mates_scattered(place, links, part, rounded, landing, ("gx", l))
     gx_ref[...] = (grad + g_ref[...].astype(F32)).astype(BF)
+
+
+class Rows:
+    def __init__(self, ref):
+        self.ref = ref
+
+    def __setitem__(self, index, value):
+        start, stop = index[0].start, index[0].stop
+        for row in range(start, stop, 48):
+            self.ref[row // PIECE, row % PIECE : row % PIECE + 48, :] = value[row - start : row - start + 48]
+
+
+def layers_kernel(
+    x_ref, g_ref, slab, slab2, small, tab, tabt, y_ref, gx_ref, wg0, sg0, sg1, piece,
+    w, middle, xg, kvb, q, ot, lse, inner, acc, top, total, part, rounded, landing,
+    g_mid, gg, dkv, do, first, second, act, slope, r1, r2, u1, u2, wg1, a1, a2, b1, b2,
+    send_sems, recv_sems, local,
+):
+    place = Place()
+    links = Links(send_sems, recv_sems)
+    loads = [load_layer(l, place, slab, slab2, w.at[l], local.at[l]) for l in (0, 1)]
+    place.greet(mates=(1, 2))
+    for l, (entry, exit_ref) in enumerate(((x_ref, middle), (middle, y_ref))):
+        forward_part(
+            l, place, links, loads[l], entry, small, tab, exit_ref, xg.at[l], kvb.at[l], q.at[l],
+            ot.at[l], lse.at[l], inner.at[l], w.at[l], acc, top, total, part, rounded.at[l],
+            landing.at[l],
+        )
+    for l, entry, exit_ref, wg, sg in ((1, g_ref, g_mid, wg1, sg1), (0, g_mid, gx_ref, wg0, sg0)):
+        upper = Scatter(place, links, wg1, slab_view, a1, a2, b1, b2, "w") if l == 0 else None
+        backward_part(
+            l, place, links, entry, xg.at[l], small, tab, tabt, kvb.at[l], q.at[l], ot.at[l],
+            lse.at[l], inner.at[l], exit_ref, Rows(wg), sg, w.at[l], gg.at[l], dkv.at[l], acc, do,
+            first, second, act, slope, part, rounded.at[2 + l], landing.at[2 + l],
+            r1.at[l], r2.at[l], u1.at[l], u2.at[l], upper, piece,
+        )
     links.finish()
 
 
@@ -825,80 +834,62 @@
     )(*args)
 
 
-def forward(l, x, slab, small, tab):
+def landing_shapes(rows, part, lead=()):
+    return [
+        pltpu.VMEM((*lead, 2, 2, 4, part, 384), BF),
+        pltpu.VMEM((*lead, 2, 2, 4, rows, 384), BF),
+        pltpu.VMEM((*lead, 2, 2, part, 384), BF),
+        pltpu.VMEM((*lead, 2, 2, rows, 384), BF),
+    ]
+
+
+def layers(*args):
+    def pair(dims, kind=BF, n=2):
+        return pltpu.VMEM((n, *dims), kind)
+
     return pl.pallas_call(
-        functools.partial(forward_kernel, l),
-        name=f"layer_{l}_forward",
+        layers_kernel,
+        name="layers",
         out_shape=(
             shape((128, 384)),
-            shape((2, ROWS, 384)),
-            shape((CHIPS, ROWS, 384)),
-            shape((3, ROWS, 128)),
-            shape((192, ROWS), F32),
-            shape((8, ROWS), F32),
-            shape((ROWS, D), F32),
+            shape((128, 384)),
+            shape((CHIPS, PIECE, D)),
+            shape((8, D), F32),
+            shape((8, D), F32),
+            shape((PIECE, D), F32),
         ),
-        in_specs=[VMEM, ANY, ANY, VMEM, VMEM],
-        out_specs=(VMEM, VMEM, ANY, VMEM, VMEM, VMEM, VMEM),
+        in_specs=[VMEM, VMEM, ANY, ANY, VMEM, VMEM, VMEM],
+        out_specs=(VMEM,) * 6,
         scratch_shapes=[
-            pltpu.VMEM((SLAB, D), BF),
-            pltpu.VMEM((2, ROWS, 384), BF),
-            pltpu.VMEM((CHIPS, ROWS, 384), BF),
+            pair((SLAB, D)),
+            pltpu.VMEM((128, 384), BF),
+            pair((2, ROWS, 384)),
+            pair((CHIPS, ROWS, 384)),
+            pair((3, ROWS, 128)),
+            pair((192, ROWS), F32),
+            pair((8, ROWS), F32),
+            pair((ROWS, D), F32),
             pltpu.VMEM((3, 128, ROWS), F32),
             pltpu.VMEM((3, 1, ROWS), F32),
             pltpu.VMEM((3, 1, ROWS), F32),
             pltpu.VMEM((2, ROWS, 384), F32),
-            pltpu.VMEM((2, ROWS, 384), BF),
-            pltpu.VMEM((3, 128, 384), BF),
-            *sems(48, 2),
-        ],
-        compiler_params=params(1 + l),
-    )(x, *slab, small, tab)
-
-
-def landing_shapes(rows, part):
-    return [
-        pltpu.VMEM((2, 2, 4, part, 384), BF),
-        pltpu.VMEM((2, 2, 4, rows, 384), BF),
-        pltpu.VMEM((2, 2, part, 384), BF),
-        pltpu.VMEM((2, 2, rows, 384), BF),
-    ]
-
-
-def backward(l, g, kept, slab, small, tab, tabt, above=()):
-    xg, kv, q, ot, lse, inner = kept
-    extra = [VMEM] if l == 0 else []
-    return pl.pallas_call(
-        functools.partial(backward_kernel, l),
-        name=f"layer_{l}_backward",
-        out_shape=(
-            shape((128, 384)),
-            shape((SLAB, D)),
-            shape((8, D), F32),
-            *([shape((PIECE, D), F32)] if l == 0 else []),
-        ),
-        in_specs=[VMEM, VMEM, ANY, ANY, VMEM, VMEM, VMEM, ANY, VMEM, VMEM, VMEM, VMEM, *([ANY] if l == 0 else [])],
-        out_specs=(VMEM, VMEM, VMEM, *extra),
-        scratch_shapes=[
-            pltpu.VMEM((SLAB, D), BF),
-            pltpu.VMEM((2, ROWS, 384), BF),
-            pltpu.VMEM((CHIPS, ROWS, 384), BF),
-            pltpu.VMEM((CHIPS, ROWS, 384), BF),
-            pltpu.VMEM((3, 128, ROWS), F32),
+            pair((2, ROWS, 384), n=4),
+            pair((3, 128, 384), n=4),
+            pltpu.VMEM((128, 384), BF),
+            pair((2, ROWS, 384)),
+            pair((CHIPS, ROWS, 384)),
             pltpu.VMEM((3, ROWS, 128), BF),
             pltpu.VMEM((ROWS, D), BF),
             pltpu.VMEM((ROWS, D), BF),
             pltpu.VMEM((ROWS, D), BF),
             pltpu.VMEM((ROWS, D), F32),
-            pltpu.VMEM((2, ROWS, 384), F32),
-            pltpu.VMEM((2, ROWS, 384), BF),
-            pltpu.VMEM((3, 128, 384), BF),
-            *landing_shapes(128, 64),
-            *sems(96, 3),
-            *([pltpu.VMEM((CHIPS, PIECE, D), BF), *landing_shapes(PIECE, 80)] if l == 0 else []),
+            *landing_shapes(128, 64, (2,)),
+            pltpu.VMEM((CHIPS, PIECE, D), BF),
+            *landing_shapes(PIECE, 80),
+            *sems(232, 2),
         ],
-        compiler_params=params(3 + l),
-    )(g, xg, *slab, small, tab, tabt, kv, q, ot, lse, inner, *above)
+        compiler_params=params(1),
+    )(*args)
 
 
 def share_grads(*args):
@@ -1051,11 +1042,7 @@
 
     x = lax.dynamic_index_in_dim(inputs, pipe, 0, keepdims=False)
     g = lax.dynamic_index_in_dim(cotangent, pipe, 0, keepdims=False)
-    middle, *kept0 = forward(0, x, slabs, smalls, tab)
-    upper, *kept1 = forward(1, middle, slabs, smalls, tab)
-    g, wg1, sg1 = backward(1, g, kept1, slabs, smalls, tab, tabt)
-    above = wg1.reshape(CHIPS, PIECE, D)
-    g, wg0, sg0, piece1 = backward(0, g, kept0, slabs, smalls, tab, tabt, (above,))
+    upper, g, wg0, sg0, sg1, piece1 = layers(x, g, *slabs, smalls, tab, tabt)
 
     lower_pipe = pipe == 0
     sent = jnp.where(lower_pipe, upper, g)
@@ -1064,7 +1051,7 @@
     boundary = jnp.stack([jnp.where(lower_pipe, held, got), jnp.where(lower_pipe, got, held)])[None]
 
     whole, sums = share_grads(
-        wg0.reshape(CHIPS, PIECE, D), piece1, sg0, sg1
+        wg0, piece1, sg0, sg1
     )
     g_qkv, g_out, g_in, g_down, g_gain, g_shift, g_qkv_b, g_out_b, g_in_b = finish(
         whole.reshape(2, SLAB, D), sums

time: 317 us -> 305 us (0.962)
  Pallas kernels: 310 us -> 297 us
    pallas_call x4 -> x1, Pallas kernels: 206 us -> 192 us  [layers(): pl.pallas_call(layers_kernel, name='layers', out_shape=(shape((128, 384))...]
  transfers between devices with their start and end apart: 1 -> 1, of which waited for: 0 -> 0; matrix products, arithmetic and copies ran while one was open for 0% -> 0% of each run, Pallas kernels for 22% -> 23%
where the time goes in v3:
time: 305 us
  Pallas kernels  297 us (97%)
  other arithmetic  3.7 us (1%)
    pallas_call x1, Pallas kernels, layers(): pl.pallas_call(layers_kernel, name='layers', out_shape=(shape((128, 384))...  192 us
    pallas_call x1, Pallas kernels, share_grads(): pl.pallas_call(grads_kernel, name='share_grads', out_shape=(shape((2, CHI...  61.6 us
    pallas_call x1, Pallas kernels, share_weights(): pl.pallas_call(weights_kernel, name='share_weights', out_shape=(shape((SL...  35.3 us
    pallas_call x1, Pallas kernels, finish(): pl.pallas_call(finish_kernel, name='finish', out_shape=(shape((3, D, 384)...  8.23 us
  transfers between devices with their start and end apart: 1, of which 0 were waited for; matrix products, arithmetic and copies ran while one was open for 0% of the time, Pallas kernels for 23%

profile of v3, /device:TPU:1, one launch (start us, length us, event | category | flops | bytes accessed | tf_op | source)
XLA Modules:
  0.0 304.7 jit_solution(12035100409895355405)
XLA Ops:
  0.6 0.0 copy-start.2
  0.7 0.0 copy-start.3
  0.7 0.1 multiply_cosine_fusion.1
  0.8 0.5 multiply_cosine_fusion
  1.4 0.2 concatenate.17
  1.7 0.2 concatenate.16
  1.9 0.6 pad_maximum_fusion.1.tabt
  2.5 0.2 concatenate.15
  2.8 0.0 copy-done.2
  2.8 0.0 copy-done.3
  2.8 0.7 dynamic-slice_bitcast_fusion
  3.5 0.8 pad_maximum_fusion.tab
  4.3 35.3 %share_weights.1 = (bf16[2304,768]{1,0:T(8,128)(2,1)}, bf16[16,144,768]{2,1,0:T(8,128)(2,1)}, bf16[2,16,768]{2,1,0:T(8,128)(2,1)}) custom-call(bf16[3,768,384]{2,1,0:T(8,128)(2,1)} %bitcast.33, bf16[384,768]{1,0:T(8,128)(2,1)} %bitcast.34, bf16[768,1536]{1,0:T(8,128)(2,1)} %bitcast.31, bf16[1536,768]{1,0:T(8,128)(2,1)} %bitcast.32, bf16[2,768]{1,0:T(2,128)(2,1)} %bitcast.39, ...), custom_call_target="tpu_custom_call" | custom-call | tf_op jit(solution)/shard_map/share_weights/pallas_call | solution.py:818
  39.6 192.1 %layers.1 = (bf16[128,384]{1,0:T(8,128)(2,1)}, bf16[128,384]{1,0:T(8,128)(2,1)}, bf16[16,144,768]{2,1,0:T(8,128)(2,1)}, f32[8,768]{1,0:T(8,128)}, f32[8,768]{1,0:T(8,128)}, /*index=5*/f32[144,768]{1,0:T(8,128)}) custom-call(bf16[128,384]{1,0:T(8,128)(2,1)} %get-tuple-element.78.x_ref, bf16[128,384]{1,0:T(8,128)(2,1)} %get-tuple-element.77.g_ref, ...), custom_call_target="tpu_custom_call" | custom-call | tf_op jit(solution)/shard_map/layers/pallas_call | solution.py:850
  231.7 0.9 broadcast_select_fusion
  232.6 0.2 collective-permute-start
  232.8 61.6 %share_grads.1 = (bf16[2,16,144,768]{3,2,1,0:T(8,128)(2,1)}, f32[2,8,768]{2,1,0:T(8,128)}) custom-call(bf16[16,144,768]{2,1,0:T(8,128)(2,1)} %get-tuple-element.35.wg0, f32[144,768]{1,0:T(8,128)} %get-tuple-element.36.piece1, f32[8,768]{1,0:T(8,128)} %get-tuple-element.37.sg0, f32[8,768]{1,0:T(8,128)} %get-tuple-element.38.sg1), custom_call_target="tpu_custom_call" | custom-call | tf_op jit(solution)/shard_map/share_grads/pallas_call | solution.py:896
  294.4 0.0 copy-start
  294.4 0.0 copy-start.1
  294.5 8.2 %finish.1 = (f32[3,768,384]{2,1,0:T(8,128)}, f32[384,768]{1,0:T(8,128)}, f32[768,1536]{1,0:T(8,128)}, f32[1536,768]{1,0:T(8,128)}, f32[2,384]{1,0:T(2,128)}, /*i...) custom-call(bf16[2,2304,768]{2,1,0:T(8,128)(2,1)} %bitcast.29, ...), custom_call_target="tpu_custom_call" | custom-call | tf_op jit(solution)/shard_map/finish/pallas_call | solution.py:985
  302.7 1.3 copy.23
  304.0 0.0 collective-permute-done
  304.0 0.0 copy-done
  304.0 0.7 maximum_bitcast_fusion
  (7 shorter events, 0.1 us)
Async XLA Ops:
  0.6 2.2 copy-start.2
  0.7 2.2 copy-start.3
  232.6 71.4 %collective-permute-start = (bf16[128,384]{1,0:T(8,128)(2,1)S(1)}, bf16[128,384]{1,0:T(8,128)(2,1)S(1)}, u32[]{:S(2)}, u32[]{:S(2)}) collective-permute-start(bf16[128,384]{1,0:T(8,128)(2,1)S(1)} %broadcast_select_fusion), channel_id=1, source_target_pairs={{0,64},{64,0},{1,65},{65,1},{2,66},{66,2},{3,67},{67,3},{4,68},{68... | collective-permute-start | bytes 294920 | tf_op jit(solution)/shard_map/ppermute | solution.py:1050
  294.4 9.6 %copy-start = (bf16[128,384]{1,0:T(8,128)(2,1)S(1)}, bf16[128,384]{1,0:T(8,128)(2,1)}, u32[]{:S(2)}) copy-start(bf16[128,384]{1,0:T(8,128)(2,1)} %get-tuple-element.34) | copy-start | bytes 294916
  294.4 9.6 %copy-start.1 = (bf16[128,384]{1,0:T(8,128)(2,1)S(1)}, bf16[128,384]{1,0:T(8,128)(2,1)}, u32[]{:S(2)}) copy-start(bf16[128,384]{1,0:T(8,128)(2,1)} %get-tuple-element.33) | copy-start | bytes 294916

commit v4 on v3

--- a/solution.py
+++ b/solution.py
@@ -528,7 +528,7 @@
 def backward_part(
     l, place, links, g_ref, xg, small, tab, tabt, kvb, q, ot, lse, inner, gx_ref, wg, sg,
     w, gg, dkv, dqt, do, first, second, act, slope, part, rounded, landing, r1, r2, u1, u2,
-    upper=None, piece=None,
+    upper=None, piece=None, ready=lambda: None,
 ):
     mates_gather(place, links, g_ref, gg, ("g", l))
     if upper is not None:
@@ -647,6 +647,7 @@
     ]
     pre = jnp.concatenate(tiles, axis=1)
     wg[KV0:Q0, :] = dot(pre, first[...], TN).astype(BF)
+    ready()
     grad_first = grad_first + dot(pre, w[KV0:Q0, :])
     sg[4:5, :] = jnp.sum(grad_first * normed, axis=0, keepdims=True)
     sg[5:6, :] = jnp.sum(grad_first, axis=0, keepdims=True)
@@ -679,15 +680,18 @@
 
 
 def layers_kernel(
-    x_ref, g_ref, slab, slab2, small, tab, tabt, y_ref, gx_ref, wg0, sg0, sg1, piece,
+    x_ref, g_ref, slab, slab2, small, tab, tabt, edge, out, out_small,
     w, middle, xg, kvb, q, ot, lse, inner, acc, top, total, part, rounded, landing,
     g_mid, gg, dkv, do, first, second, act, slope, r1, r2, u1, u2, wg1, a1, a2, b1, b2,
-    send_sems, recv_sems, local,
+    ends, wg0, sg0, sg1, piece1, c1, c2, d1, d2, buf, piece, got, sm, along_x, along_z, across,
+    beside, send_sems, recv_sems, local,
 ):
     place = Place()
     links = Links(send_sems, recv_sems)
+    y_ref, gx_ref = ends.at[0], ends.at[1]
+    lower = Scatter(place, links, wg0, slab_view, c1, c2, d1, d2, "w0")
     loads = [load_layer(l, place, slab, slab2, w.at[l], local.at[l]) for l in (0, 1)]
-    place.greet(mates=(1, 2))
+    place.greet(mates=(1, 2, 3), partner=True, far=True)
     for l, (entry, exit_ref) in enumerate(((x_ref, middle), (middle, y_ref))):
         forward_part(
             l, place, links, loads[l], entry, small, tab, exit_ref, xg.at[l], kvb.at[l], q.at[l],
@@ -700,20 +704,26 @@
             l, place, links, entry, xg.at[l], small, tab, tabt, kvb.at[l], q.at[l], ot.at[l],
             lse.at[l], inner.at[l], exit_ref, Rows(wg), sg, w.at[l], gg.at[l], dkv.at[l], acc, do,
             first, second, act, slope, part, rounded.at[2 + l], landing.at[2 + l],
-            r1.at[l], r2.at[l], u1.at[l], u2.at[l], upper, piece,
+            r1.at[l], r2.at[l], u1.at[l], u2.at[l], upper, piece1,
+            lower.begin if l == 0 else lambda: None,
         )
+    lower_pipe = place.pipe == 0
+    ends[2] = jnp.where(lower_pipe, ends[0], ends[1])
+    edge[place.pipe] = jnp.where(lower_pipe, ends[1], ends[0])
+    links.send("edge", lambda: (ends.at[2], ends.at[3], place.partner()))
+    grads_part(
+        place, links, lower, sg0, sg1, piece1, out, out_small, buf, piece, got,
+        sm, along_x, along_z, across, beside, local,
+    )
+    links.arrived("edge", ends.at[3], place.partner())
+    edge[1 - place.pipe] = ends[3]
     links.finish()
 
 
-def grads_kernel(
-    wg0, piece1, sg0, sg1, out, out_small, buf, own, piece, got, r1, r2, u1, u2,
-    sm, along_x, along_z, across, beside, send_sems, recv_sems, local
+def grads_part(
+    place, links, scatter, sg0, sg1, piece1, out, out_small, buf, piece, got,
+    sm, along_x, along_z, across, beside, local,
 ):
-    place = Place()
-    links = Links(send_sems, recv_sems)
-    load = pltpu.make_async_copy(wg0, own, local.at[0])
-    load.start()
-    place.greet(mates=(1, 2, 3), partner=True, far=True)
     sm[0, 0] = sg0[...]
     sm[0, 1] = sg1[...]
     for d in (1, 2, 3):
@@ -752,9 +762,6 @@
         out_small[place.core] = jnp.where(norm, total, sm[3, 0])
         out_small[1 - place.core] = jnp.where(norm, total, beside[0])
 
-    load.wait()
-    scatter = Scatter(place, links, own, slab_view, r1, r2, u1, u2)
-    scatter.begin()
     small_z()
     scatter.middle()
     small_pipe()
@@ -786,16 +793,15 @@
 
     parts = [Gather(place, links, buf.at[place.core], part_view(i), i) for i in range(2)]
     gather_parts(parts, whole, pass_on)
-    keep = pltpu.make_async_copy(buf.at[place.core], out.at[place.core], local.at[0])
+    keep = pltpu.make_async_copy(buf.at[place.core], out.at[place.core], local.at[2])
     keep.start()
     small_last()
     for a, b in ((0, 0), *ORDER_F):
         links.arrived(("core", a, b), buf.at[1 - place.core, place.slot(a, b)], sibling)
-    rest = pltpu.make_async_copy(buf.at[1 - place.core], out.at[1 - place.core], local.at[1])
+    rest = pltpu.make_async_copy(buf.at[1 - place.core], out.at[1 - place.core], local.at[3])
     rest.start()
     keep.wait()
     rest.wait()
-    links.finish()
 
 
 VMEM = pl.BlockSpec(memory_space=pltpu.VMEM)
@@ -811,7 +817,7 @@
 
 
 def params(i):
-    return pltpu.CompilerParams(collective_id=i, has_side_effects=True, vmem_limit_bytes=56 * 2**20)
+    return pltpu.CompilerParams(collective_id=i, has_side_effects=True, vmem_limit_bytes=62 * 2**20)
 
 
 def share_weights(*args):
@@ -850,16 +856,9 @@
     return pl.pallas_call(
         layers_kernel,
         name="layers",
-        out_shape=(
-            shape((128, 384)),
-            shape((128, 384)),
-            shape((CHIPS, PIECE, D)),
-            shape((8, D), F32),
-            shape((8, D), F32),
-            shape((PIECE, D), F32),
-        ),
+        out_shape=(shape((2, 128, 384)), shape((2, CHIPS, PIECE, D)), shape((2, 8, D), F32)),
         in_specs=[VMEM, VMEM, ANY, ANY, VMEM, VMEM, VMEM],
-        out_specs=(VMEM,) * 6,
+        out_specs=(VMEM, ANY, VMEM),
         scratch_shapes=[
             pair((SLAB, D)),
             pltpu.VMEM((128, 384), BF),
@@ -886,33 +885,23 @@
             *landing_shapes(128, 64, (2,)),
             pltpu.VMEM((CHIPS, PIECE, D), BF),
             *landing_shapes(PIECE, 80),
-            *sems(232, 2),
-        ],
-        compiler_params=params(1),
-    )(*args)
-
-
-def share_grads(*args):
-    return pl.pallas_call(
-        grads_kernel,
-        name="share_grads",
-        out_shape=(shape((2, CHIPS, PIECE, D)), shape((2, 8, D), F32)),
-        in_specs=[ANY, VMEM, VMEM, VMEM],
-        out_specs=(ANY, VMEM),
-        scratch_shapes=[
+            pltpu.VMEM((4, 128, 384), BF),
+            pltpu.VMEM((CHIPS, PIECE, D), BF),
+            pltpu.VMEM((8, D), F32),
+            pltpu.VMEM((8, D), F32),
+            pltpu.VMEM((PIECE, D), F32),
+            *landing_shapes(PIECE, 80),
             pltpu.VMEM((2, CHIPS, PIECE, D), BF),
-            pltpu.VMEM((CHIPS, PIECE, D), BF),
             pltpu.VMEM((PIECE, D), F32),
             pltpu.VMEM((2, PIECE, D), BF),
-            *landing_shapes(PIECE, 80),
             pltpu.VMEM((4, 2, 8, D), F32),
             pltpu.VMEM((3, 2, 8, D), F32),
             pltpu.VMEM((3, 2, 8, D), F32),
             pltpu.VMEM((8, D), F32),
             pltpu.VMEM((3, 8, D), F32),
-            *sems(176, 2),
+            *sems(376, 4),
         ],
-        compiler_params=params(5),
+        compiler_params=params(1),
     )(*args)
 
 
@@ -1042,22 +1031,12 @@
 
     x = lax.dynamic_index_in_dim(inputs, pipe, 0, keepdims=False)
     g = lax.dynamic_index_in_dim(cotangent, pipe, 0, keepdims=False)
-    upper, g, wg0, sg0, sg1, piece1 = layers(x, g, *slabs, smalls, tab, tabt)
-
-    lower_pipe = pipe == 0
-    sent = jnp.where(lower_pipe, upper, g)
-    held = jnp.where(lower_pipe, g, upper)
-    got = lax.ppermute(sent, "pipe", [(0, 1), (1, 0)])
-    boundary = jnp.stack([jnp.where(lower_pipe, held, got), jnp.where(lower_pipe, got, held)])[None]
-
-    whole, sums = share_grads(
-        wg0, piece1, sg0, sg1
-    )
+    edge, whole, sums = layers(x, g, *slabs, smalls, tab, tabt)
     g_qkv, g_out, g_in, g_down, g_gain, g_shift, g_qkv_b, g_out_b, g_in_b = finish(
         whole.reshape(2, SLAB, D), sums
     )
     return (
-        boundary,
+        edge[None],
         g_gain[None],
         g_shift[None],
         g_qkv[None],

time: 305 us -> 298 us (0.977)
  Pallas kernels: 297 us -> 291 us
    pallas_call x2 -> x1, Pallas kernels: 254 us -> 247 us  [layers(): pl.pallas_call(layers_kernel, name='layers', out_shape=(shape((2, 128, 38...]
  transfers between devices with their start and end apart: 1 -> 0, of which waited for: 0 -> 0; matrix products, arithmetic and copies ran while one was open for 0% -> 0% of each run, Pallas kernels for 23% -> 0%
where the time goes in v4:
time: 298 us
  Pallas kernels  291 us (98%)
  local copies, waits for them, and re-layouts  4.38 us (1%)
    pallas_call x1, Pallas kernels, layers(): pl.pallas_call(layers_kernel, name='layers', out_shape=(shape((2, 128, 38...  247 us
    pallas_call x1, Pallas kernels, share_weights(): pl.pallas_call(weights_kernel, name='share_weights', out_shape=(shape((SL...  35.4 us
    pallas_call x1, Pallas kernels, finish(): pl.pallas_call(finish_kernel, name='finish', out_shape=(shape((3, D, 384)...  8.23 us

profile of v4, /device:TPU:1, one launch (start us, length us, event | category | flops | bytes accessed | tf_op | source)
XLA Modules:
  0.0 297.8 jit_solution(1207229632682801173)
XLA Ops:
  0.7 0.1 multiply_cosine_fusion.1
  0.8 0.6 pad_maximum_fusion.1.tabt
  1.4 1.6 dynamic-slice_bitcast_fusion
  3.0 0.5 multiply_cosine_fusion
  3.6 0.2 concatenate.15
  3.9 0.2 concatenate.17
  4.2 0.2 concatenate.16
  4.4 0.8 pad_maximum_fusion.tab
  5.2 35.4 %share_weights.1 = (bf16[2304,768]{1,0:T(8,128)(2,1)}, bf16[16,144,768]{2,1,0:T(8,128)(2,1)}, bf16[2,16,768]{2,1,0:T(8,128)(2,1)}) custom-call(bf16[3,768,384]{2,1,0:T(8,128)(2,1)} %bitcast.28, bf16[384,768]{1,0:T(8,128)(2,1)} %bitcast.29, bf16[768,1536]{1,0:T(8,128)(2,1)} %bitcast.26, bf16[1536,768]{1,0:T(8,128)(2,1)} %bitcast.27, bf16[2,768]{1,0:T(2,128)(2,1)} %bitcast.35, ...), custom_call_target="tpu_custom_call" | custom-call | tf_op jit(solution)/shard_map/share_weights/pallas_call | solution.py:824
  40.6 247.0 %layers.1 = (bf16[2,128,384]{2,1,0:T(8,128)(2,1)}, bf16[2,16,144,768]{3,2,1,0:T(8,128)(2,1)}, f32[2,8,768]{2,1,0:T(8,128)}) custom-call(bf16[128,384]{1,0:T(8,128)(2,1)} %get-tuple-element.66.x_ref, bf16[128,384]{1,0:T(8,128)(2,1)} %get-tuple-element.65.g_ref, bf16[2304,768]{1,0:T(8,128)(2,1)} %get-tuple-element.25.slab, bf16[2304,768]{1,0:T(8,128)(2,1)} %bitcast.25, ...), custom_call_target="tpu_custom_call" | custom-call | tf_op jit(solution)/shard_map/layers/pallas_call | solution.py:856
  287.6 0.0 copy-start
  287.6 8.2 %finish.1 = (f32[3,768,384]{2,1,0:T(8,128)}, f32[384,768]{1,0:T(8,128)}, f32[768,1536]{1,0:T(8,128)}, f32[1536,768]{1,0:T(8,128)}, f32[2,384]{1,0:T(2,128)}, /*i...) custom-call(bf16[2,2304,768]{2,1,0:T(8,128)(2,1)} %bitcast.24, ...), custom_call_target="tpu_custom_call" | custom-call | tf_op jit(solution)/shard_map/finish/pallas_call | solution.py:974
  295.8 1.3 copy.23
  297.1 0.0 copy-done
  297.1 0.7 copy.25
  (5 shorter events, 0.0 us)
Async XLA Ops:
  287.6 9.5 %copy-start = (bf16[2,128,384]{2,1,0:T(8,128)(2,1)S(1)}, bf16[2,128,384]{2,1,0:T(8,128)(2,1)}, u32[]{:S(2)}) copy-start(bf16[2,128,384]{2,1,0:T(8,128)(2,1)} %get-tuple-element.28) | copy-start | bytes 589828
